TPU v7x, 512 devices: a whole 4x4x16 slice. The times are simulated.
512 devices in a mesh: section: 32 (over y, x, core), expert: 16 (over z).
Axes of the slice: x: 4, y: 4, z: 16, core: 2. Of those that a mesh axis runs over, the one named last changes fastest.
Arguments:
- inputs_down: bfloat16 [32, 1024, 3584], P('section', 'expert'), may hold values from -6 to 6
- inputs_up: bfloat16 [32, 1024, 3584], P('section', 'expert'), may hold values from -6 to 6
- routes_down: int32 [32, 1024, 1], P('section', 'expert'), may hold values from 0 to 1; in each aligned block of 64 rows (0 to 63, 64 to 127, ..., all dimensions but the last counted through in order) at most 34 rows name the same one
- routes_up: int32 [32, 1024, 1], P('section', 'expert'), may hold values from 0 to 1; in each aligned block of 64 rows (0 to 63, 64 to 127, ..., all dimensions but the last counted through in order) at most 34 rows name the same one
- probs_down: float32 [32, 1024, 1], P('section', 'expert'), may hold values from 0.5 to 1.5
- probs_up: float32 [32, 1024, 1], P('section', 'expert'), may hold values from 0.5 to 1.5
- norm_gain: float32 [32, 3584], P('section'), may hold values from 0.1 to 1.9
- gate_weight: bfloat16 [32, 3584, 2048], P('section', None, 'expert'), may hold values from -0.09375 to 0.09375
- up_weight: bfloat16 [32, 3584, 2048], P('section', None, 'expert'), may hold values from -0.09375 to 0.09375
- down_weight: bfloat16 [32, 2048, 3584], P('section', 'expert'), may hold values from -0.1875 to 0.1875
Outputs:
- outputs_down: bfloat16 [32, 1024, 3584], P('section', 'expert')
- outputs_up: bfloat16 [32, 1024, 3584], P('section', 'expert')
Inputs may be any that keep to these rules, and one draw needn't show every extreme that they name: `routes_down`: among the tokens of one device, each expert is named by at most 34 tokens, a bound that some block reaches. `routes_up`: among the tokens of one device, each expert is named by at most 34 tokens, a bound that some block reaches.
All inputs are finite; a program needn't handle non-finite values.
Results may differ from a plain program's by a relative error of at most 0.0053.
Values may be sent and summed in bfloat16 or wider, within the bound.
No kernel may reach another device: no remote copies, remote signals or barrier semaphores. Data moves between devices by JAX's collectives and lax.ppermute only.
A program may use at most 128 MiB of HBM per device.

v0:
```python
import jax
import jax.numpy as jnp
from jax import lax
from jax.sharding import PartitionSpec as P

EXP_SECTION = 2
CAP = 34


def passed_along(block, axis, distance):
    devices = range(lax.axis_size(axis))
    route = [((i - distance) % len(devices), i) for i in devices]
    return lax.ppermute(block, axis, route)


def norm_rows(inputs, gain):
    values = inputs.astype(jnp.float32)
    meansq = jnp.mean(values * values, axis=-1, keepdims=True) + 1e-06
    return (values * lax.rsqrt(meansq) * gain[None, :]).astype(jnp.bfloat16)


def expert_rows(blocks, gate_cols, up_cols, down_rows):
    flat = blocks.reshape(-1, blocks.shape[-1])
    gate = jnp.dot(flat, gate_cols, preferred_element_type=jnp.float32)
    upper = jnp.dot(flat, up_cols, preferred_element_type=jnp.float32)
    hidden = (jax.nn.silu(gate) * upper).astype(jnp.bfloat16)
    parts = jnp.dot(hidden, down_rows, preferred_element_type=jnp.float32).astype(jnp.bfloat16)
    return parts.reshape(blocks.shape[:-1] + (down_rows.shape[1],))


def selection(picks, expert_id):
    chosen = (picks == expert_id).astype(jnp.int32)
    places = jnp.cumsum(chosen) - 1
    slots = jnp.arange(CAP, dtype=jnp.int32)
    return ((places[None, :] == slots[:, None]) & (chosen[None, :] > 0)).astype(jnp.bfloat16)


def own_slot(picks):
    table = (picks[:, None] == jnp.arange(EXP_SECTION, dtype=jnp.int32)[None, :]).astype(jnp.int32)
    places = jnp.cumsum(table, axis=0) - 1
    return picks * CAP + jnp.sum(table * places, axis=1)


def return_partial(parts):
    return lax.all_to_all(parts, "expert", split_axis=0, concat_axis=0, tiled=True)


def per_device(
    inputs_down,
    inputs_up,
    routes_down,
    routes_up,
    probs_down,
    probs_up,
    norm_gain,
    gate_weight,
    up_weight,
    down_weight,
):
    gate_cols = gate_weight[0]
    up_cols = up_weight[0]
    down_rows = down_weight[0]
    gain = norm_gain[0]
    shards = lax.axis_size("expert") // EXP_SECTION

    def apply_expert(blocks):
        return expert_rows(blocks, gate_cols, up_cols, down_rows)

    def dispatch(normed, picks):
        buffers = jnp.stack(
            [
                jnp.dot(
                    selection(picks, expert_id), normed, preferred_element_type=jnp.float32
                ).astype(jnp.bfloat16)
                for expert_id in range(EXP_SECTION)
            ]
        )
        sending = jnp.repeat(buffers, shards, axis=0)
        return apply_expert(
            lax.all_to_all(sending, "expert", split_axis=0, concat_axis=0, tiled=True)
        )

    def combine(returned, inputs, picks, weights_in):
        totals = returned.astype(jnp.float32).reshape(EXP_SECTION, shards, CAP, returned.shape[-1])
        totals = jnp.sum(totals, axis=1).reshape(EXP_SECTION * CAP, returned.shape[-1])
        gathered = jnp.take(totals, own_slot(picks), axis=0)
        moved = inputs.astype(jnp.float32) + weights_in[:, None] * gathered
        return moved.astype(jnp.bfloat16)

    acts_down = inputs_down[0]
    acts_up = inputs_up[0]
    picks_down = routes_down[0, :, 0]
    picks_up = routes_up[0, :, 0]
    back_down = return_partial(dispatch(norm_rows(acts_down, gain), picks_down))
    moved_down = combine(back_down, acts_down, picks_down, probs_down[0, :, 0])
    back_up = return_partial(dispatch(norm_rows(acts_up, gain), picks_up))
    moved_up = combine(back_up, acts_up, picks_up, probs_up[0, :, 0])
    next_down = passed_along(moved_down, "section", 1)
    next_up = passed_along(moved_up, "section", -1)
    return (next_down[None], next_up[None])


def solution(mesh):
    in_specs = (
        P("section", "expert", None),
        P("section", "expert", None),
        P("section", "expert", None),
        P("section", "expert", None),
        P("section", "expert", None),
        P("section", "expert", None),
        P("section", None),
        P("section", None, "expert"),
        P("section", None, "expert"),
        P("section", "expert", None),
    )
    out_specs = (P("section", "expert", None), P("section", "expert", None))
    return jax.shard_map(
        per_device, mesh=mesh, in_specs=in_specs, out_specs=out_specs, check_vma=False
    )
```

profile of v0, /device:TPU:1, one launch (start us, length us, event | category | flops | bytes accessed | tf_op | source)
XLA Modules:
  0.0 875.1 jit_solution(16653028365894885907)
XLA Ops:
  2.2 0.8 select_reduce_fusion
  4.0 1.2 fusion.10
  6.3 1.3 fusion.2
  7.7 1.3 fusion.3
  9.1 2.4 broadcast_in_dim.19
  11.4 15.9 %all-to-all-start.2 = ((bf16[16,34,3584]{2,1,0:T(8,128)(2,1)}), bf16[16,34,3584]{2,1,0:T(8,128)(2,1)}, u32[]{:S(2)}, u32[]{:S(2)}) async-start(bf16[16,34,3584]{2,1,0:T(8,128)(2,1)} %bitcast.73), calls=%async_computation.2 | async-start | bytes 9175040 | tf_op jit(solution)/shard_map/all_to_all | solution.py:80
  29.3 196.7 %all-to-all-done.2 = bf16[16,34,3584]{2,1,0:T(8,128)(2,1)} async-done(((bf16[16,34,3584]{2,1,0:T(8,128)(2,1)}), bf16[16,34,3584]{2,1,0:T(8,128)(2,1)}, u32[]{:S(2)}, u32[]{:S(2)}) %all-to-all-start.2) | async-done | bytes 3899424 | tf_op jit(solution)/shard_map/all_to_all | solution.py:80
  226.0 2.5 broadcast_in_dim.17
  228.5 11.2 %all-to-all-start = ((bf16[16,34,3584]{2,1,0:T(8,128)(2,1)}), bf16[16,34,3584]{2,1,0:T(8,128)(2,1)}, u32[]{:S(2)}, u32[]{:S(2)}) async-start(bf16[16,34,3584]{2,1,0:T(8,128)(2,1)} %bitcast.74), calls=%async_computation | async-start | bytes 9175040 | tf_op jit(solution)/shard_map/all_to_all | solution.py:80
  239.8 5.2 reshape.268
  245.0 3.3 fusion.20
  248.4 8.1 convolution_convert_fusion
  256.5 5.3 reshape.269
  261.8 176.6 %all-to-all-done = bf16[16,34,3584]{2,1,0:T(8,128)(2,1)} async-done(((bf16[16,34,3584]{2,1,0:T(8,128)(2,1)}), bf16[16,34,3584]{2,1,0:T(8,128)(2,1)}, u32[]{:S(2)}, u32[]{:S(2)}) %all-to-all-start) | async-done | bytes 3899424 | tf_op jit(solution)/shard_map/all_to_all | solution.py:80
  438.4 11.2 %all-to-all-start.3 = ((bf16[16,34,3584]{2,1,0:T(8,128)(2,1)}), bf16[16,34,3584]{2,1,0:T(8,128)(2,1)}, u32[]{:S(2)}, u32[]{:S(2)}) async-start(bf16[16,34,3584]{2,1,0:T(8,128)(2,1)} %reshape.269), calls=%async_computation.3 | async-start | bytes 9175040 | tf_op jit(solution)/shard_map/all_to_all | solution.py:45
  449.7 5.2 reshape.262
  454.8 3.3 fusion.22
  458.1 8.1 convolution_convert_fusion.1
  466.2 5.2 reshape.263
  471.4 176.9 %all-to-all-done.3 = bf16[16,34,3584]{2,1,0:T(8,128)(2,1)} async-done(((bf16[16,34,3584]{2,1,0:T(8,128)(2,1)}), bf16[16,34,3584]{2,1,0:T(8,128)(2,1)}, u32[]{:S(2)}, u32[]{:S(2)}) %all-to-all-start.3) | async-done | bytes 3899424 | tf_op jit(solution)/shard_map/all_to_all | solution.py:45
  648.3 11.2 %all-to-all-start.1 = ((bf16[16,34,3584]{2,1,0:T(8,128)(2,1)}), bf16[16,34,3584]{2,1,0:T(8,128)(2,1)}, u32[]{:S(2)}, u32[]{:S(2)}) async-start(bf16[16,34,3584]{2,1,0:T(8,128)(2,1)} %reshape.263), calls=%async_computation.1 | async-start | bytes 9175040 | tf_op jit(solution)/shard_map/all_to_all | solution.py:45
  659.6 3.1 convert_reduce_fusion
  662.8 0.9 gather_fusion.1
  663.8 1.0 fusion.13
  664.8 2.7 collective-permute-start.1
  667.5 190.7 %all-to-all-done.1 = bf16[16,34,3584]{2,1,0:T(8,128)(2,1)} async-done(((bf16[16,34,3584]{2,1,0:T(8,128)(2,1)}), bf16[16,34,3584]{2,1,0:T(8,128)(2,1)}, u32[]{:S(2)}, u32[]{:S(2)}) %all-to-all-start.1) | async-done | bytes 3899424 | tf_op jit(solution)/shard_map/all_to_all | solution.py:45
  858.2 3.1 convert_reduce_fusion.1
  861.5 0.9 gather_fusion
  862.7 4.4 collective-permute-start
  867.1 5.4 collective-permute-done
  872.5 0.8 copy.22
  873.3 1.8 copy.23
  (53 shorter events, 6.2 us)
Async XLA Ops:
  0.6 247.8 %copy-start = (bf16[1,128,3584]{2,1,0:T(8,128)(2,1)S(1)}, bf16[1,128,3584]{2,1,0:T(8,128)(2,1)}, u32[]{:S(2)}) copy-start(bf16[1,128,3584]{2,1,0:T(8,128)(2,1)} %param.21) | copy-start | bytes 2752516
  11.4 15.9 %copy-start.5 = (s32[1,64,1]{1,2,0:T(1,128)S(1)}, s32[1,64,1]{1,2,0:T(1,128)}, u32[]{:S(2)}) copy-start(s32[1,64,1]{1,2,0:T(1,128)} %param.14) | copy-start | bytes 772
  11.4 16.9 %copy-start.3 = (bf16[1,64,3584]{2,1,0:T(8,128)(2,1)S(1)}, bf16[1,64,3584]{2,1,0:T(8,128)(2,1)}, u32[]{:S(2)}) copy-start(bf16[1,64,3584]{2,1,0:T(8,128)(2,1)} %param.12) | copy-start | bytes 1376260
  11.4 214.6 %all-to-all-start.2 = ((bf16[16,34,3584]{2,1,0:T(8,128)(2,1)}), bf16[16,34,3584]{2,1,0:T(8,128)(2,1)}, u32[]{:S(2)}, u32[]{:S(2)}) async-start(bf16[16,34,3584]{2,1,0:T(8,128)(2,1)} %bitcast.73), calls=%async_computation.2 | async-start | bytes 9175040 | tf_op jit(solution)/shard_map/all_to_all | solution.py:80
  228.5 209.9 %all-to-all-start = ((bf16[16,34,3584]{2,1,0:T(8,128)(2,1)}), bf16[16,34,3584]{2,1,0:T(8,128)(2,1)}, u32[]{:S(2)}, u32[]{:S(2)}) async-start(bf16[16,34,3584]{2,1,0:T(8,128)(2,1)} %bitcast.74), calls=%async_computation | async-start | bytes 9175040 | tf_op jit(solution)/shard_map/all_to_all | solution.py:80
  239.8 5.3 copy-start.8
  245.0 3.4 copy-start.1
  438.4 209.9 %all-to-all-start.3 = ((bf16[16,34,3584]{2,1,0:T(8,128)(2,1)}), bf16[16,34,3584]{2,1,0:T(8,128)(2,1)}, u32[]{:S(2)}, u32[]{:S(2)}) async-start(bf16[16,34,3584]{2,1,0:T(8,128)(2,1)} %reshape.269), calls=%async_computation.3 | async-start | bytes 9175040 | tf_op jit(solution)/shard_map/all_to_all | solution.py:45
  648.3 209.9 %all-to-all-start.1 = ((bf16[16,34,3584]{2,1,0:T(8,128)(2,1)}), bf16[16,34,3584]{2,1,0:T(8,128)(2,1)}, u32[]{:S(2)}, u32[]{:S(2)}) async-start(bf16[16,34,3584]{2,1,0:T(8,128)(2,1)} %reshape.263), calls=%async_computation.1 | async-start | bytes 9175040 | tf_op jit(solution)/shard_map/all_to_all | solution.py:45
  662.8 1.0 copy-start.2
  662.8 1.0 copy-start.6
  664.8 202.3 %collective-permute-start.1 = (bf16[64,3584]{1,0:T(8,128)(2,1)}, bf16[64,3584]{1,0:T(8,128)(2,1)}, u32[]{:S(2)}, u32[]{:S(2)}) collective-permute-start(bf16[64,3584]{1,0:T(8,128)(2,1)} %fusion.13), channel_id=1, source_target_pairs={{16,0},{32,16},{48,32},{64,48},{80,64},{96,80},{112,96},{128,112},... | collective-permute-start | bytes 1376264 | tf_op jit(solution)/shard_map/ppermute | solution.py:13
  861.4 1.0 copy-start.4
  861.5 1.0 copy-start.7
  862.7 9.8 %collective-permute-start = (bf16[64,3584]{1,0:T(8,128)(2,1)S(1)}, bf16[64,3584]{1,0:T(8,128)(2,1)S(1)}, u32[]{:S(2)}, u32[]{:S(2)}) collective-permute-start(bf16[64,3584]{1,0:T(8,128)(2,1)S(1)} %fusion.9), channel_id=1, source_target_pairs={{496,0},{0,16},{16,32},{32,48},{48,64},{64,80},{80,96},{96,112},{1... | collective-permute-start | bytes 1376264 | tf_op jit(solution)/shard_map/ppermute | solution.py:13
where the time goes:
time: 880 us; the launch traced here: 875 us
  waiting for transfers between devices  746 us (85%)
  starting transfers between devices  56.7 us (6%)
  local copies, waits for them, and re-layouts  30.9 us (4%)
  matrix products  26.2 us (3%)
  other arithmetic  13.9 us (2%)
    all_to_all x2, waiting for transfers between devices, dispatch(): lax.all_to_all(sending, 'expert', split_axis=0, concat_axis=0, tiled=True)  373 us
    all_to_all x2, waiting for transfers between devices, return_partial(): lax.all_to_all(parts, 'expert', split_axis=0, concat_axis=0, tiled=True)  368 us
    all_to_all x2, starting transfers between devices, dispatch(): lax.all_to_all(sending, 'expert', split_axis=0, concat_axis=0, tiled=True)  27.2 us
    all_to_all x2, starting transfers between devices, return_partial(): lax.all_to_all(parts, 'expert', split_axis=0, concat_axis=0, tiled=True)  22.4 us
  transfers between devices with their start and end apart: 6, of which 5 were waited for; matrix products, arithmetic and copies ran while one was open for 6% of the time, Pallas kernels for 0%

commit v1 on v0

v1 whole, which is shorter than its diff:
```python
import jax
import jax.numpy as jnp
from jax import lax
from jax.experimental import pallas as pl
from jax.experimental.pallas import tpu as pltpu
from jax.sharding import PartitionSpec as P

EXP_SECTION = 2
TAIL = 128
VMEM_LIMIT = 48 * 1024 * 1024


def call(kernel, out_shape, flops, moved, **options):
    return pl.pallas_call(
        kernel,
        out_shape=out_shape,
        cost_estimate=pl.CostEstimate(flops=flops, bytes_accessed=moved, transcendentals=0),
        compiler_params=pltpu.CompilerParams(vmem_limit_bytes=VMEM_LIMIT),
        **options,
    )


def norm_rows(inputs, gain, tail=None):
    rows, width = inputs.shape
    extra = 0 if tail is None else tail.shape[1]

    def kernel(inputs_ref, gain_ref, *refs):
        values = inputs_ref[...].astype(jnp.float32)
        meansq = jnp.mean(values * values, axis=-1, keepdims=True) + 1e-06
        refs[-1][:, :width] = (values * lax.rsqrt(meansq) * gain_ref[...]).astype(jnp.bfloat16)
        if extra:
            refs[-1][:, width:] = refs[0][...]

    shape = jax.ShapeDtypeStruct((rows, width + extra), jnp.bfloat16)
    operands = (inputs, gain) + (() if tail is None else (tail,))
    return call(kernel, shape, 4 * rows * width, 4 * rows * width)(*operands)


def hidden_of(tokens, gate_up):
    units = gate_up.shape[1] // 2
    both = jnp.dot(tokens, gate_up, preferred_element_type=jnp.float32)
    gated, upper = both[:, :units], both[:, units:]
    return gated / (1.0 + jnp.exp(-gated)) * upper


def hidden_rows(blocks, carriers, lanes, expert, gate_up):
    count = len(blocks)
    width, units = gate_up.shape[0], gate_up.shape[1] // 2
    rows = blocks[0].shape[0]
    given = []
    for block in list(blocks) + list(carriers):
        if not any(block is other for other in given):
            given.append(block)
    place = [[block is other for other in given].index(True) for block in blocks]
    bearer = [[block is other for other in given].index(True) for block in carriers]

    def kernel(expert_ref, gate_up_ref, *refs):
        mine = expert_ref[0].astype(jnp.float32)
        for i in range(count):
            hidden = hidden_of(refs[place[i]][:, :width], gate_up_ref[...])
            picks = refs[bearer[i]][:, lanes[i] : lanes[i] + 1].astype(jnp.float32)
            refs[len(given) + i][...] = jnp.where(picks == mine, hidden, 0.0).astype(
                jnp.bfloat16
            )

    shape = [jax.ShapeDtypeStruct((rows, units), jnp.bfloat16)] * count
    flops = 4 * count * rows * width * units
    vmem = pl.BlockSpec(memory_space=pltpu.VMEM)
    return call(
        kernel,
        shape,
        flops,
        4 * width * units + 2 * count * rows * width,
        in_specs=[pl.BlockSpec(memory_space=pltpu.SMEM)] + [vmem] * (1 + len(given)),
    )(expert, gate_up, *given)


def add_partial(hidden, down, arrived):
    def kernel(hidden_ref, down_ref, *refs):
        total = jnp.dot(hidden_ref[...], down_ref[...], preferred_element_type=jnp.float32)
        if arrived is not None:
            total = total + refs[0][...].astype(jnp.float32)
        refs[-1][...] = total.astype(jnp.bfloat16)

    rows, units = hidden.shape
    width = down.shape[1]
    shape = jax.ShapeDtypeStruct((rows, width), jnp.bfloat16)
    operands = (hidden, down) + (() if arrived is None else (arrived,))
    return call(kernel, shape, 2 * rows * units * width, 2 * units * width + 4 * rows * width)(
        *operands
    )


def finish(hidden, down, arrived, inputs, weights_in):
    def kernel(hidden_ref, down_ref, a_ref, b_ref, inputs_ref, weights_ref, out_ref):
        total = jnp.dot(hidden_ref[...], down_ref[...], preferred_element_type=jnp.float32)
        total = total + a_ref[...].astype(jnp.float32) + b_ref[...].astype(jnp.float32)
        moved = inputs_ref[...].astype(jnp.float32) + weights_ref[...] * total
        out_ref[...] = moved.astype(jnp.bfloat16)

    rows, width = inputs.shape
    shape = jax.ShapeDtypeStruct((rows, width), jnp.bfloat16)
    return call(kernel, shape, 2 * rows * hidden.shape[1] * width, 8 * rows * width)(
        hidden, down, *arrived, inputs, weights_in
    )


def per_device(
    inputs_down,
    inputs_up,
    routes_down,
    routes_up,
    probs_down,
    probs_up,
    norm_gain,
    gate_weight,
    up_weight,
    down_weight,
):
    down = down_weight[0]
    gate_up = jnp.concatenate([gate_weight[0], up_weight[0]], axis=1)
    acts_down, acts_up = inputs_down[0], inputs_up[0]
    rows, width = acts_down.shape
    ring = lax.axis_size("expert")
    half = ring // 2
    me = lax.axis_index("expert")
    my_expert = me // (ring // EXP_SECTION)
    forward = [(i, (i + 1) % ring) for i in range(ring)]
    backward = [(i, (i - 1) % ring) for i in range(ring)]

    expert = my_expert.astype(jnp.int32).reshape(1)

    picks = jnp.concatenate([routes_down[0], routes_up[0]], axis=1).astype(jnp.bfloat16)
    tail = jnp.repeat(picks, TAIL // 2, axis=1)
    lanes = (width, width + TAIL // 2)
    normed = (norm_rows(acts_down, norm_gain, tail), norm_rows(acts_up, norm_gain))

    hidden = [{}, {}]
    hidden[0][0], hidden[1][0] = hidden_rows(
        normed, (normed[0], normed[0]), lanes, expert, gate_up
    )
    ahead, behind = list(normed), list(normed)
    for step in range(1, half + 1):
        for way in range(2):
            if step < half or way == 0:
                ahead[way] = lax.ppermute(ahead[way], "expert", backward)
            if step < half or way == 1:
                behind[way] = lax.ppermute(behind[way], "expert", forward)
            if 1 < step < half:
                ahead[way], hidden[way][step - 1] = lax.optimization_barrier(
                    (ahead[way], hidden[way][step - 1])
                )
                behind[way], hidden[way][1 - step] = lax.optimization_barrier(
                    (behind[way], hidden[way][1 - step])
                )
        if step < half:
            (
                hidden[0][step],
                hidden[1][step],
                hidden[0][-step],
                hidden[1][-step],
            ) = hidden_rows(
                (ahead[0], ahead[1], behind[0], behind[1]),
                (ahead[0], ahead[0], behind[0], behind[0]),
                lanes * 2,
                expert,
                gate_up,
            )
        else:
            hidden[0][half], hidden[1][-half] = hidden_rows(
                (ahead[0], behind[1]), (ahead[0], ahead[0]), lanes, expert, gate_up
            )

    def add(way, offset, arrived):
        return add_partial(hidden[way][offset], down, arrived)

    onward, returning = [None, None], [None, None]
    for step in range(half, 0, -1):
        for way in range(2):
            if step < half or way == 0:
                onward[way] = lax.ppermute(add(way, step, onward[way]), "expert", forward)
            if step < half or way == 1:
                returning[way] = lax.ppermute(
                    add(way, -step, returning[way]), "expert", backward
                )
    moved_down, moved_up = (
        finish(hidden[way][0], down, (onward[way], returning[way]), acts, probs)
        for way, acts, probs in ((0, acts_down, probs_down[0]), (1, acts_up, probs_up[0]))
    )

    sections = lax.axis_size("section")
    next_down = lax.ppermute(
        moved_down, "section", [(i, (i + 1) % sections) for i in range(sections)]
    )
    next_up = lax.ppermute(
        moved_up, "section", [(i, (i - 1) % sections) for i in range(sections)]
    )
    return (next_down[None], next_up[None])


def solution(mesh):
    in_specs = (
        P("section", "expert", None),
        P("section", "expert", None),
        P("section", "expert", None),
        P("section", "expert", None),
        P("section", "expert", None),
        P("section", "expert", None),
        P("section", None),
        P("section", None, "expert"),
        P("section", None, "expert"),
        P("section", "expert", None),
    )
    out_specs = (P("section", "expert", None), P("section", "expert", None))
    return jax.shard_map(
        per_device, mesh=mesh, in_specs=in_specs, out_specs=out_specs, check_vma=False
    )
```

time: 880 us -> 342 us (0.39)
  waiting for transfers between devices: 746 us -> 91.9 us
  starting transfers between devices: 56.7 us -> 209 us
  Pallas kernels: 0 us -> 27.4 us
  matrix products: 26.2 us -> 0 us
  local copies, waits for them, and re-layouts: 30.9 us -> 6.78 us
  other arithmetic: 13.9 us -> 2.34 us
    all_to_all x4 -> x0, waiting for transfers between devices: 741 us -> none  [the longest x2 373 us: dispatch(): lax.all_to_all(sending, 'expert', split_axis=0, concat_axis=0, tiled=True)]
    ppermute x2 -> x62, starting transfers between devices: 7.11 us -> 209 us  [the longest x15 78.4 us: per_device(): ahead[way] = lax.ppermute(ahead[way], 'expert', backward)]
    ppermute x2 -> x62, waiting for transfers between devices: 5.39 us -> 91.9 us  [the longest x15 45.9 us: per_device(): onward[way] = lax.ppermute(add(way, step, onward[way]), 'expert', forward)]
    all_to_all x4 -> x0, starting transfers between devices: 49.6 us -> none  [the longest x2 27.2 us: dispatch(): lax.all_to_all(sending, 'expert', split_axis=0, concat_axis=0, tiled=True)]
    pallas_call x0 -> x43, Pallas kernels: none -> 27.4 us  [the longest x9 12.6 us: hidden_rows(): call(kernel, shape, flops, 4 * width * units + 2 * count * rows * width,...]
    dot_general x8 -> x0, matrix products: 26.2 us -> none  [the longest x2 16.3 us: expert_rows(): jnp.dot(hidden, down_rows, preferred_element_type=jnp.float32)]
    reshape x6 -> x1, local copies, waits for them, and re-layouts: 21 us -> 0.09 us  [per_device(): tail = jnp.repeat(picks, TAIL // 2, axis=1)]
  transfers between devices with their start and end apart: 6 -> 62, of which waited for: 5 -> 38; matrix products, arithmetic and copies ran while one was open for 6% -> 1% of each run, Pallas kernels for 0% -> 8%
where the time goes in v1:
time: 342 us; the launch traced here: 339 us
  starting transfers between devices  209 us (61%)
  waiting for transfers between devices  91.9 us (27%)
  Pallas kernels  27.4 us (8%)
  local copies, waits for them, and re-layouts  6.78 us (2%)
    ppermute x15, starting transfers between devices, per_device(): ahead[way] = lax.ppermute(ahead[way], 'expert', backward)  78.4 us
    ppermute x15, starting transfers between devices, per_device(): lax.ppermute(add(way, -step, returning[way]), 'expert', backward)  50.2 us
    ppermute x15, waiting for transfers between devices, per_device(): onward[way] = lax.ppermute(add(way, step, onward[way]), 'expert', forward)  45.9 us
    ppermute x15, starting transfers between devices, per_device(): onward[way] = lax.ppermute(add(way, step, onward[way]), 'expert', forward)  35.2 us
    ppermute x15, starting transfers between devices, per_device(): behind[way] = lax.ppermute(behind[way], 'expert', forward)  30.1 us
    ppermute x15, waiting for transfers between devices, per_device(): behind[way] = lax.ppermute(behind[way], 'expert', forward)  24.1 us
    ppermute x15, waiting for transfers between devices, per_device(): ahead[way] = lax.ppermute(ahead[way], 'expert', backward)  14.2 us
    pallas_call x9, Pallas kernels, hidden_rows(): call(kernel, shape, flops, 4 * width * units + 2 * count * rows * width,...  12.6 us
  transfers between devices with their start and end apart: 62, of which 38 were waited for; matrix products, arithmetic and copies ran while one was open for 1% of the time, Pallas kernels for 8%

profile of v1, /device:TPU:1, one launch (start us, length us, event | category | flops | bytes accessed | tf_op | source)
XLA Modules:
  0.0 338.7 jit_solution(2086333026219751678)
XLA Ops:
  3.6 12.0 %collective-permute-start = (bf16[64,3712]{1,0:T(8,128)(2,1)S(1)}, bf16[64,3712]{1,0:T(8,128)(2,1)}, u32[]{:S(2)}, u32[]{:S(2)}) collective-permute-start(bf16[64,3712]{1,0:T(8,128)(2,1)S(1)} %shard_map.113.refs_0_), channel_id=1, source_target_pairs={{0,15},{1,0},{2,1},{3,2},{4,3},{5,4},{6,5},{7,6},{8,7},{9,8},{10,9... | collective-permute-start | bytes 1425416 | tf_op jit(solution)/shard_map/ppermute | solution.py:146
  19.5 4.6 %collective-permute-start.2 = (bf16[64,3584]{1,0:T(8,128)(2,1)S(1)}, bf16[64,3584]{1,0:T(8,128)(2,1)S(1)}, u32[]{:S(2)}, u32[]{:S(2)}) collective-permute-start(bf16[64,3584]{1,0:T(8,128)(2,1)S(1)} %shard_map.114.refs_1_), channel_id=1, source_target_pairs={{0,15},{1,0},{2,1},{3,2},{4,3},{5,4},{6,5},{7,6},{8,7},{9,8},{10,9... | collective-permute-start | bytes 1376264 | tf_op jit(solution)/shard_map/ppermute | solution.py:146
  26.0 5.8 %collective-permute-done.4.refs_3_ = bf16[64,3584]{1,0:T(8,128)(2,1)} collective-permute-done((bf16[64,3584]{1,0:T(8,128)(2,1)S(1)}, bf16[64,3584]{1,0:T(8,128)(2,1)}, u32[]{:S(2)}, u32[]{:S(2)}) %collective-permute-start.4) | collective-permute-done | bytes 458784 | tf_op jit(solution)/shard_map/ppermute | solution.py:148
  33.7 4.6 %collective-permute-start.1 = (bf16[64,3712]{1,0:T(8,128)(2,1)}, bf16[64,3712]{1,0:T(8,128)(2,1)S(1)}, u32[]{:S(2)}, u32[]{:S(2)}) collective-permute-start(bf16[64,3712]{1,0:T(8,128)(2,1)} %collective-permute-done.refs_0_), channel_id=1, source_target_pairs={{0,15},{1,0},{2,1},{3,2},{4,3},{5,4},{6,5},{7,6},{8,7},{9,8},{10,9... | collective-permute-start | bytes 1425416 | tf_op jit(solution)/shard_map/ppermute | solution.py:146
  54.9 5.3 %collective-permute-start.10 = (bf16[64,3584]{1,0:T(8,128)(2,1)S(1)}, bf16[64,3584]{1,0:T(8,128)(2,1)S(1)}, u32[]{:S(2)}, u32[]{:S(2)}) collective-permute-start(bf16[64,3584]{1,0:T(8,128)(2,1)S(1)} %collective-permute-done.6.refs_1_), channel_id=1, source_target_pairs={{0,15},{1,0},{2,1},{3,2},{4,3},{5,4},{6,5},{7,6},{8,7},{9,8},{10,9... | collective-permute-start | bytes 1376264 | tf_op jit(solution)/shard_map/ppermute | solution.py:146
  65.2 5.2 %collective-permute-start.9 = (bf16[64,3712]{1,0:T(8,128)(2,1)S(1)}, bf16[64,3712]{1,0:T(8,128)(2,1)S(1)}, u32[]{:S(2)}, u32[]{:S(2)}) collective-permute-start(bf16[64,3712]{1,0:T(8,128)(2,1)S(1)} %collective-permute-done.5.refs_0_), channel_id=1, source_target_pairs={{0,15},{1,0},{2,1},{3,2},{4,3},{5,4},{6,5},{7,6},{8,7},{9,8},{10,9... | collective-permute-start | bytes 1425416 | tf_op jit(solution)/shard_map/ppermute | solution.py:146
  74.9 5.3 %collective-permute-start.14 = (bf16[64,3584]{1,0:T(8,128)(2,1)S(1)}, bf16[64,3584]{1,0:T(8,128)(2,1)S(1)}, u32[]{:S(2)}, u32[]{:S(2)}) collective-permute-start(bf16[64,3584]{1,0:T(8,128)(2,1)S(1)} %collective-permute-done.10.refs_1_), channel_id=1, source_target_pairs={{0,15},{1,0},{2,1},{3,2},{4,3},{5,4},{6,5},{7,6},{8,7},{9,8},{10,9... | collective-permute-start | bytes 1376264 | tf_op jit(solution)/shard_map/ppermute | solution.py:146
  85.1 5.3 %collective-permute-start.13 = (bf16[64,3712]{1,0:T(8,128)(2,1)S(1)}, bf16[64,3712]{1,0:T(8,128)(2,1)S(1)}, u32[]{:S(2)}, u32[]{:S(2)}) collective-permute-start(bf16[64,3712]{1,0:T(8,128)(2,1)S(1)} %collective-permute-done.9.refs_0_), channel_id=1, source_target_pairs={{0,15},{1,0},{2,1},{3,2},{4,3},{5,4},{6,5},{7,6},{8,7},{9,8},{10,9... | collective-permute-start | bytes 1425416 | tf_op jit(solution)/shard_map/ppermute | solution.py:146
  94.9 5.3 %collective-permute-start.18 = (bf16[64,3584]{1,0:T(8,128)(2,1)S(1)}, bf16[64,3584]{1,0:T(8,128)(2,1)S(1)}, u32[]{:S(2)}, u32[]{:S(2)}) collective-permute-start(bf16[64,3584]{1,0:T(8,128)(2,1)S(1)} %collective-permute-done.14.refs_1_), channel_id=1, source_target_pairs={{0,15},{1,0},{2,1},{3,2},{4,3},{5,4},{6,5},{7,6},{8,7},{9,8},{10,9... | collective-permute-start | bytes 1376264 | tf_op jit(solution)/shard_map/ppermute | solution.py:146
  105.1 5.3 %collective-permute-start.17 = (bf16[64,3712]{1,0:T(8,128)(2,1)S(1)}, bf16[64,3712]{1,0:T(8,128)(2,1)S(1)}, u32[]{:S(2)}, u32[]{:S(2)}) collective-permute-start(bf16[64,3712]{1,0:T(8,128)(2,1)S(1)} %collective-permute-done.13.refs_0_), channel_id=1, source_target_pairs={{0,15},{1,0},{2,1},{3,2},{4,3},{5,4},{6,5},{7,6},{8,7},{9,8},{10,9... | collective-permute-start | bytes 1425416 | tf_op jit(solution)/shard_map/ppermute | solution.py:146
  114.9 5.3 %collective-permute-start.22 = (bf16[64,3584]{1,0:T(8,128)(2,1)S(1)}, bf16[64,3584]{1,0:T(8,128)(2,1)S(1)}, u32[]{:S(2)}, u32[]{:S(2)}) collective-permute-start(bf16[64,3584]{1,0:T(8,128)(2,1)S(1)} %collective-permute-done.18.refs_1_), channel_id=1, source_target_pairs={{0,15},{1,0},{2,1},{3,2},{4,3},{5,4},{6,5},{7,6},{8,7},{9,8},{10,9... | collective-permute-start | bytes 1376264 | tf_op jit(solution)/shard_map/ppermute | solution.py:146
  125.1 5.3 %collective-permute-start.21 = (bf16[64,3712]{1,0:T(8,128)(2,1)S(1)}, bf16[64,3712]{1,0:T(8,128)(2,1)S(1)}, u32[]{:S(2)}, u32[]{:S(2)}) collective-permute-start(bf16[64,3712]{1,0:T(8,128)(2,1)S(1)} %collective-permute-done.17.refs_0_), channel_id=1, source_target_pairs={{0,15},{1,0},{2,1},{3,2},{4,3},{5,4},{6,5},{7,6},{8,7},{9,8},{10,9... | collective-permute-start | bytes 1425416 | tf_op jit(solution)/shard_map/ppermute | solution.py:146
  134.9 6.2 %collective-permute-done.23.refs_2_ = bf16[64,3712]{1,0:T(8,128)(2,1)S(1)} collective-permute-done((bf16[64,3712]{1,0:T(8,128)(2,1)S(1)}, bf16[64,3712]{1,0:T(8,128)(2,1)S(1)}, u32[]{:S(2)}, u32[]{:S(2)}) %collective-permute-start.23) | collective-permute-done | bytes 475168 | tf_op jit(solution)/shard_map/ppermute | solution.py:148
  145.1 5.3 %collective-permute-start.28 = (bf16[64,3712]{1,0:T(8,128)(2,1)S(1)}, bf16[64,3712]{1,0:T(8,128)(2,1)S(1)}, u32[]{:S(2)}, u32[]{:S(2)}) collective-permute-start(bf16[64,3712]{1,0:T(8,128)(2,1)S(1)} %collective-permute-done.21.refs_0_), channel_id=1, source_target_pairs={{0,15},{1,0},{2,1},{3,2},{4,3},{5,4},{6,5},{7,6},{8,7},{9,8},{10,9... | collective-permute-start | bytes 1425416 | tf_op jit(solution)/shard_map/ppermute | solution.py:146
  154.8 4.6 %collective-permute-start.25 = (bf16[64,3584]{1,0:T(8,128)(2,1)S(1)}, bf16[64,3584]{1,0:T(8,128)(2,1)S(1)}, u32[]{:S(2)}, u32[]{:S(2)}) collective-permute-start(bf16[64,3584]{1,0:T(8,128)(2,1)S(1)} %collective-permute-done.22.refs_1_), channel_id=1, source_target_pairs={{0,15},{1,0},{2,1},{3,2},{4,3},{5,4},{6,5},{7,6},{8,7},{9,8},{10,9... | collective-permute-start | bytes 1376264 | tf_op jit(solution)/shard_map/ppermute | solution.py:146
  165.0 4.6 %collective-permute-start.53 = (bf16[64,3584]{1,0:T(8,128)(2,1)S(1)}, bf16[64,3584]{1,0:T(8,128)(2,1)S(1)}, u32[]{:S(2)}, u32[]{:S(2)}) collective-permute-start(bf16[64,3584]{1,0:T(8,128)(2,1)S(1)} %shard_map.147), channel_id=1, source_target_pairs={{0,15},{1,0},{2,1},{3,2},{4,3},{5,4},{6,5},{7,6},{8,7},{9,8},{10,9... | collective-permute-start | bytes 1376264 | tf_op jit(solution)/shard_map/ppermute | solution.py:183
  175.8 3.4 collective-permute-start.46
  184.3 4.8 %collective-permute-start.54 = (bf16[64,3584]{1,0:T(8,128)(2,1)S(1)}, bf16[64,3584]{1,0:T(8,128)(2,1)S(1)}, u32[]{:S(2)}, u32[]{:S(2)}) collective-permute-start(bf16[64,3584]{1,0:T(8,128)(2,1)S(1)} %shard_map.148), channel_id=1, source_target_pairs={{0,15},{1,0},{2,1},{3,2},{4,3},{5,4},{6,5},{7,6},{8,7},{9,8},{10,9... | collective-permute-start | bytes 1376264 | tf_op jit(solution)/shard_map/ppermute | solution.py:183
  194.9 5.7 %collective-permute-done.31.refs_0_ = bf16[64,3584]{1,0:T(8,128)(2,1)S(1)} collective-permute-done((bf16[64,3584]{1,0:T(8,128)(2,1)S(1)}, bf16[64,3584]{1,0:T(8,128)(2,1)S(1)}, u32[]{:S(2)}, u32[]{:S(2)}) %collective-permute-start.31) | collective-permute-done | bytes 458784 | tf_op jit(solution)/shard_map/ppermute | solution.py:181
  203.1 4.6 %collective-permute-start.55 = (bf16[64,3584]{1,0:T(8,128)(2,1)S(1)}, bf16[64,3584]{1,0:T(8,128)(2,1)S(1)}, u32[]{:S(2)}, u32[]{:S(2)}) collective-permute-start(bf16[64,3584]{1,0:T(8,128)(2,1)S(1)} %shard_map.149), channel_id=1, source_target_pairs={{0,15},{1,0},{2,1},{3,2},{4,3},{5,4},{6,5},{7,6},{8,7},{9,8},{10,9... | collective-permute-start | bytes 1376264 | tf_op jit(solution)/shard_map/ppermute | solution.py:183
  213.6 6.7 %collective-permute-done.32.refs_0_ = bf16[64,3584]{1,0:T(8,128)(2,1)S(1)} collective-permute-done((bf16[64,3584]{1,0:T(8,128)(2,1)S(1)}, bf16[64,3584]{1,0:T(8,128)(2,1)S(1)}, u32[]{:S(2)}, u32[]{:S(2)}) %collective-permute-start.32) | collective-permute-done | bytes 458784 | tf_op jit(solution)/shard_map/ppermute | solution.py:181
  222.8 4.6 %collective-permute-start.56 = (bf16[64,3584]{1,0:T(8,128)(2,1)S(1)}, bf16[64,3584]{1,0:T(8,128)(2,1)S(1)}, u32[]{:S(2)}, u32[]{:S(2)}) collective-permute-start(bf16[64,3584]{1,0:T(8,128)(2,1)S(1)} %shard_map.150), channel_id=1, source_target_pairs={{0,15},{1,0},{2,1},{3,2},{4,3},{5,4},{6,5},{7,6},{8,7},{9,8},{10,9... | collective-permute-start | bytes 1376264 | tf_op jit(solution)/shard_map/ppermute | solution.py:183
  233.2 6.7 %collective-permute-done.33.refs_0_ = bf16[64,3584]{1,0:T(8,128)(2,1)S(1)} collective-permute-done((bf16[64,3584]{1,0:T(8,128)(2,1)S(1)}, bf16[64,3584]{1,0:T(8,128)(2,1)S(1)}, u32[]{:S(2)}, u32[]{:S(2)}) %collective-permute-start.33) | collective-permute-done | bytes 458784 | tf_op jit(solution)/shard_map/ppermute | solution.py:181
  242.4 4.6 %collective-permute-start.57 = (bf16[64,3584]{1,0:T(8,128)(2,1)S(1)}, bf16[64,3584]{1,0:T(8,128)(2,1)S(1)}, u32[]{:S(2)}, u32[]{:S(2)}) collective-permute-start(bf16[64,3584]{1,0:T(8,128)(2,1)S(1)} %shard_map.151), channel_id=1, source_target_pairs={{0,15},{1,0},{2,1},{3,2},{4,3},{5,4},{6,5},{7,6},{8,7},{9,8},{10,9... | collective-permute-start | bytes 1376264 | tf_op jit(solution)/shard_map/ppermute | solution.py:183
  252.9 6.7 %collective-permute-done.34.refs_0_ = bf16[64,3584]{1,0:T(8,128)(2,1)S(1)} collective-permute-done((bf16[64,3584]{1,0:T(8,128)(2,1)S(1)}, bf16[64,3584]{1,0:T(8,128)(2,1)S(1)}, u32[]{:S(2)}, u32[]{:S(2)}) %collective-permute-start.34) | collective-permute-done | bytes 458784 | tf_op jit(solution)/shard_map/ppermute | solution.py:181
  262.1 4.6 %collective-permute-start.58 = (bf16[64,3584]{1,0:T(8,128)(2,1)S(1)}, bf16[64,3584]{1,0:T(8,128)(2,1)S(1)}, u32[]{:S(2)}, u32[]{:S(2)}) collective-permute-start(bf16[64,3584]{1,0:T(8,128)(2,1)S(1)} %shard_map.152), channel_id=1, source_target_pairs={{0,15},{1,0},{2,1},{3,2},{4,3},{5,4},{6,5},{7,6},{8,7},{9,8},{10,9... | collective-permute-start | bytes 1376264 | tf_op jit(solution)/shard_map/ppermute | solution.py:183
  272.6 6.7 %collective-permute-done.35.refs_0_ = bf16[64,3584]{1,0:T(8,128)(2,1)S(1)} collective-permute-done((bf16[64,3584]{1,0:T(8,128)(2,1)S(1)}, bf16[64,3584]{1,0:T(8,128)(2,1)S(1)}, u32[]{:S(2)}, u32[]{:S(2)}) %collective-permute-start.35) | collective-permute-done | bytes 458784 | tf_op jit(solution)/shard_map/ppermute | solution.py:181
  281.8 4.6 %collective-permute-start.59 = (bf16[64,3584]{1,0:T(8,128)(2,1)S(1)}, bf16[64,3584]{1,0:T(8,128)(2,1)S(1)}, u32[]{:S(2)}, u32[]{:S(2)}) collective-permute-start(bf16[64,3584]{1,0:T(8,128)(2,1)S(1)} %shard_map.153), channel_id=1, source_target_pairs={{0,15},{1,0},{2,1},{3,2},{4,3},{5,4},{6,5},{7,6},{8,7},{9,8},{10,9... | collective-permute-start | bytes 1376264 | tf_op jit(solution)/shard_map/ppermute | solution.py:183
  290.4 8.5 %collective-permute-done.36.refs_0_ = bf16[64,3584]{1,0:T(8,128)(2,1)S(1)} collective-permute-done((bf16[64,3584]{1,0:T(8,128)(2,1)S(1)}, bf16[64,3584]{1,0:T(8,128)(2,1)S(1)}, u32[]{:S(2)}, u32[]{:S(2)}) %collective-permute-start.36) | collective-permute-done | bytes 458784 | tf_op jit(solution)/shard_map/ppermute | solution.py:181
  304.9 4.6 %collective-permute-start.60 = (bf16[64,3584]{1,0:T(8,128)(2,1)}, bf16[64,3584]{1,0:T(8,128)(2,1)}, u32[]{:S(2)}, u32[]{:S(2)}) collective-permute-start(bf16[64,3584]{1,0:T(8,128)(2,1)} %shard_map.154), channel_id=1, source_target_pairs={{0,15},{1,0},{2,1},{3,2},{4,3},{5,4},{6,5},{7,6},{8,7},{9,8},{10,9... | collective-permute-start | bytes 1376264 | tf_op jit(solution)/shard_map/ppermute | solution.py:183
  313.3 12.5 %collective-permute-start.45 = (bf16[64,3584]{1,0:T(8,128)(2,1)S(1)}, bf16[64,3584]{1,0:T(8,128)(2,1)S(1)}, u32[]{:S(2)}, u32[]{:S(2)}) collective-permute-start(bf16[64,3584]{1,0:T(8,128)(2,1)S(1)} %shard_map.139), channel_id=1, source_target_pairs={{0,16},{16,32},{32,48},{48,64},{64,80},{80,96},{96,112},{112,128},... | collective-permute-start | bytes 1376264 | tf_op jit(solution)/shard_map/ppermute | solution.py:192
  331.2 6.0 %collective-permute-done.61 = bf16[64,3584]{1,0:T(8,128)(2,1)S(1)} collective-permute-done((bf16[64,3584]{1,0:T(8,128)(2,1)S(1)}, bf16[64,3584]{1,0:T(8,128)(2,1)S(1)}, u32[]{:S(2)}, u32[]{:S(2)}) %collective-permute-start.61) | collective-permute-done | bytes 458784 | tf_op jit(solution)/shard_map/ppermute | solution.py:195
  (167 shorter events, 152.1 us)
Async XLA Ops:
  3.6 30.1 %collective-permute-start = (bf16[64,3712]{1,0:T(8,128)(2,1)S(1)}, bf16[64,3712]{1,0:T(8,128)(2,1)}, u32[]{:S(2)}, u32[]{:S(2)}) collective-permute-start(bf16[64,3712]{1,0:T(8,128)(2,1)S(1)} %shard_map.113.refs_0_), channel_id=1, source_target_pairs={{0,15},{1,0},{2,1},{3,2},{4,3},{5,4},{6,5},{7,6},{8,7},{9,8},{10,9... | collective-permute-start | bytes 1425416 | tf_op jit(solution)/shard_map/ppermute | solution.py:146
  19.5 20.5 %collective-permute-start.2 = (bf16[64,3584]{1,0:T(8,128)(2,1)S(1)}, bf16[64,3584]{1,0:T(8,128)(2,1)S(1)}, u32[]{:S(2)}, u32[]{:S(2)}) collective-permute-start(bf16[64,3584]{1,0:T(8,128)(2,1)S(1)} %shard_map.114.refs_1_), channel_id=1, source_target_pairs={{0,15},{1,0},{2,1},{3,2},{4,3},{5,4},{6,5},{7,6},{8,7},{9,8},{10,9... | collective-permute-start | bytes 1376264 | tf_op jit(solution)/shard_map/ppermute | solution.py:146
  31.8 19.9 %collective-permute-start.8 = (bf16[64,3584]{1,0:T(8,128)(2,1)}, bf16[64,3584]{1,0:T(8,128)(2,1)S(1)}, u32[]{:S(2)}, u32[]{:S(2)}) collective-permute-start(bf16[64,3584]{1,0:T(8,128)(2,1)} %collective-permute-done.4.refs_3_), channel_id=1, source_target_pairs={{0,1},{1,2},{2,3},{3,4},{4,5},{5,6},{6,7},{7,8},{8,9},{9,10},{10,1... | collective-permute-start | bytes 1376264 | tf_op jit(solution)/shard_map/ppermute | solution.py:148
  42.0 19.9 %collective-permute-start.7 = (bf16[64,3712]{1,0:T(8,128)(2,1)}, bf16[64,3712]{1,0:T(8,128)(2,1)S(1)}, u32[]{:S(2)}, u32[]{:S(2)}) collective-permute-start(bf16[64,3712]{1,0:T(8,128)(2,1)} %collective-permute-done.3.refs_2_), channel_id=1, source_target_pairs={{0,1},{1,2},{2,3},{3,4},{4,5},{5,6},{6,7},{7,8},{8,9},{9,10},{10,1... | collective-permute-start | bytes 1425416 | tf_op jit(solution)/shard_map/ppermute | solution.py:148
  54.9 20.0 %collective-permute-start.10 = (bf16[64,3584]{1,0:T(8,128)(2,1)S(1)}, bf16[64,3584]{1,0:T(8,128)(2,1)S(1)}, u32[]{:S(2)}, u32[]{:S(2)}) collective-permute-start(bf16[64,3584]{1,0:T(8,128)(2,1)S(1)} %collective-permute-done.6.refs_1_), channel_id=1, source_target_pairs={{0,15},{1,0},{2,1},{3,2},{4,3},{5,4},{6,5},{7,6},{8,7},{9,8},{10,9... | collective-permute-start | bytes 1376264 | tf_op jit(solution)/shard_map/ppermute | solution.py:146
  65.2 19.9 %collective-permute-start.9 = (bf16[64,3712]{1,0:T(8,128)(2,1)S(1)}, bf16[64,3712]{1,0:T(8,128)(2,1)S(1)}, u32[]{:S(2)}, u32[]{:S(2)}) collective-permute-start(bf16[64,3712]{1,0:T(8,128)(2,1)S(1)} %collective-permute-done.5.refs_0_), channel_id=1, source_target_pairs={{0,15},{1,0},{2,1},{3,2},{4,3},{5,4},{6,5},{7,6},{8,7},{9,8},{10,9... | collective-permute-start | bytes 1425416 | tf_op jit(solution)/shard_map/ppermute | solution.py:146
  70.9 20.0 %collective-permute-start.16 = (bf16[64,3584]{1,0:T(8,128)(2,1)S(1)}, bf16[64,3584]{1,0:T(8,128)(2,1)S(1)}, u32[]{:S(2)}, u32[]{:S(2)}) collective-permute-start(bf16[64,3584]{1,0:T(8,128)(2,1)S(1)} %collective-permute-done.12.refs_3_), channel_id=1, source_target_pairs={{0,1},{1,2},{2,3},{3,4},{4,5},{5,6},{6,7},{7,8},{8,9},{9,10},{10,1... | collective-permute-start | bytes 1376264 | tf_op jit(solution)/shard_map/ppermute | solution.py:148
  74.9 20.0 %collective-permute-start.14 = (bf16[64,3584]{1,0:T(8,128)(2,1)S(1)}, bf16[64,3584]{1,0:T(8,128)(2,1)S(1)}, u32[]{:S(2)}, u32[]{:S(2)}) collective-permute-start(bf16[64,3584]{1,0:T(8,128)(2,1)S(1)} %collective-permute-done.10.refs_1_), channel_id=1, source_target_pairs={{0,15},{1,0},{2,1},{3,2},{4,3},{5,4},{6,5},{7,6},{8,7},{9,8},{10,9... | collective-permute-start | bytes 1376264 | tf_op jit(solution)/shard_map/ppermute | solution.py:146
  81.1 20.0 %collective-permute-start.15 = (bf16[64,3712]{1,0:T(8,128)(2,1)S(1)}, bf16[64,3712]{1,0:T(8,128)(2,1)S(1)}, u32[]{:S(2)}, u32[]{:S(2)}) collective-permute-start(bf16[64,3712]{1,0:T(8,128)(2,1)S(1)} %collective-permute-done.11.refs_2_), channel_id=1, source_target_pairs={{0,1},{1,2},{2,3},{3,4},{4,5},{5,6},{6,7},{7,8},{8,9},{9,10},{10,1... | collective-permute-start | bytes 1425416 | tf_op jit(solution)/shard_map/ppermute | solution.py:148
  85.1 20.0 %collective-permute-start.13 = (bf16[64,3712]{1,0:T(8,128)(2,1)S(1)}, bf16[64,3712]{1,0:T(8,128)(2,1)S(1)}, u32[]{:S(2)}, u32[]{:S(2)}) collective-permute-start(bf16[64,3712]{1,0:T(8,128)(2,1)S(1)} %collective-permute-done.9.refs_0_), channel_id=1, source_target_pairs={{0,15},{1,0},{2,1},{3,2},{4,3},{5,4},{6,5},{7,6},{8,7},{9,8},{10,9... | collective-permute-start | bytes 1425416 | tf_op jit(solution)/shard_map/ppermute | solution.py:146
  90.9 20.0 %collective-permute-start.20 = (bf16[64,3584]{1,0:T(8,128)(2,1)S(1)}, bf16[64,3584]{1,0:T(8,128)(2,1)S(1)}, u32[]{:S(2)}, u32[]{:S(2)}) collective-permute-start(bf16[64,3584]{1,0:T(8,128)(2,1)S(1)} %collective-permute-done.16.refs_3_), channel_id=1, source_target_pairs={{0,1},{1,2},{2,3},{3,4},{4,5},{5,6},{6,7},{7,8},{8,9},{9,10},{10,1... | collective-permute-start | bytes 1376264 | tf_op jit(solution)/shard_map/ppermute | solution.py:148
  94.9 20.0 %collective-permute-start.18 = (bf16[64,3584]{1,0:T(8,128)(2,1)S(1)}, bf16[64,3584]{1,0:T(8,128)(2,1)S(1)}, u32[]{:S(2)}, u32[]{:S(2)}) collective-permute-start(bf16[64,3584]{1,0:T(8,128)(2,1)S(1)} %collective-permute-done.14.refs_1_), channel_id=1, source_target_pairs={{0,15},{1,0},{2,1},{3,2},{4,3},{5,4},{6,5},{7,6},{8,7},{9,8},{10,9... | collective-permute-start | bytes 1376264 | tf_op jit(solution)/shard_map/ppermute | solution.py:146
  101.1 20.0 %collective-permute-start.19 = (bf16[64,3712]{1,0:T(8,128)(2,1)S(1)}, bf16[64,3712]{1,0:T(8,128)(2,1)S(1)}, u32[]{:S(2)}, u32[]{:S(2)}) collective-permute-start(bf16[64,3712]{1,0:T(8,128)(2,1)S(1)} %collective-permute-done.15.refs_2_), channel_id=1, source_target_pairs={{0,1},{1,2},{2,3},{3,4},{4,5},{5,6},{6,7},{7,8},{8,9},{9,10},{10,1... | collective-permute-start | bytes 1425416 | tf_op jit(solution)/shard_map/ppermute | solution.py:148
  105.1 20.0 %collective-permute-start.17 = (bf16[64,3712]{1,0:T(8,128)(2,1)S(1)}, bf16[64,3712]{1,0:T(8,128)(2,1)S(1)}, u32[]{:S(2)}, u32[]{:S(2)}) collective-permute-start(bf16[64,3712]{1,0:T(8,128)(2,1)S(1)} %collective-permute-done.13.refs_0_), channel_id=1, source_target_pairs={{0,15},{1,0},{2,1},{3,2},{4,3},{5,4},{6,5},{7,6},{8,7},{9,8},{10,9... | collective-permute-start | bytes 1425416 | tf_op jit(solution)/shard_map/ppermute | solution.py:146
  110.9 20.0 %collective-permute-start.24 = (bf16[64,3584]{1,0:T(8,128)(2,1)S(1)}, bf16[64,3584]{1,0:T(8,128)(2,1)S(1)}, u32[]{:S(2)}, u32[]{:S(2)}) collective-permute-start(bf16[64,3584]{1,0:T(8,128)(2,1)S(1)} %collective-permute-done.20.refs_3_), channel_id=1, source_target_pairs={{0,1},{1,2},{2,3},{3,4},{4,5},{5,6},{6,7},{7,8},{8,9},{9,10},{10,1... | collective-permute-start | bytes 1376264 | tf_op jit(solution)/shard_map/ppermute | solution.py:148
  114.9 20.0 %collective-permute-start.22 = (bf16[64,3584]{1,0:T(8,128)(2,1)S(1)}, bf16[64,3584]{1,0:T(8,128)(2,1)S(1)}, u32[]{:S(2)}, u32[]{:S(2)}) collective-permute-start(bf16[64,3584]{1,0:T(8,128)(2,1)S(1)} %collective-permute-done.18.refs_1_), channel_id=1, source_target_pairs={{0,15},{1,0},{2,1},{3,2},{4,3},{5,4},{6,5},{7,6},{8,7},{9,8},{10,9... | collective-permute-start | bytes 1376264 | tf_op jit(solution)/shard_map/ppermute | solution.py:146
  121.1 20.0 %collective-permute-start.23 = (bf16[64,3712]{1,0:T(8,128)(2,1)S(1)}, bf16[64,3712]{1,0:T(8,128)(2,1)S(1)}, u32[]{:S(2)}, u32[]{:S(2)}) collective-permute-start(bf16[64,3712]{1,0:T(8,128)(2,1)S(1)} %collective-permute-done.19.refs_2_), channel_id=1, source_target_pairs={{0,1},{1,2},{2,3},{3,4},{4,5},{5,6},{6,7},{7,8},{8,9},{9,10},{10,1... | collective-permute-start | bytes 1425416 | tf_op jit(solution)/shard_map/ppermute | solution.py:148
  125.1 20.0 %collective-permute-start.21 = (bf16[64,3712]{1,0:T(8,128)(2,1)S(1)}, bf16[64,3712]{1,0:T(8,128)(2,1)S(1)}, u32[]{:S(2)}, u32[]{:S(2)}) collective-permute-start(bf16[64,3712]{1,0:T(8,128)(2,1)S(1)} %collective-permute-done.17.refs_0_), channel_id=1, source_target_pairs={{0,15},{1,0},{2,1},{3,2},{4,3},{5,4},{6,5},{7,6},{8,7},{9,8},{10,9... | collective-permute-start | bytes 1425416 | tf_op jit(solution)/shard_map/ppermute | solution.py:146
  130.9 20.0 %collective-permute-start.27 = (bf16[64,3584]{1,0:T(8,128)(2,1)S(1)}, bf16[64,3584]{1,0:T(8,128)(2,1)S(1)}, u32[]{:S(2)}, u32[]{:S(2)}) collective-permute-start(bf16[64,3584]{1,0:T(8,128)(2,1)S(1)} %collective-permute-done.24.refs_3_), channel_id=1, source_target_pairs={{0,1},{1,2},{2,3},{3,4},{4,5},{5,6},{6,7},{7,8},{8,9},{9,10},{10,1... | collective-permute-start | bytes 1376264 | tf_op jit(solution)/shard_map/ppermute | solution.py:148
  200.9 19.4 %collective-permute-start.32 = (bf16[64,3584]{1,0:T(8,128)(2,1)S(1)}, bf16[64,3584]{1,0:T(8,128)(2,1)S(1)}, u32[]{:S(2)}, u32[]{:S(2)}) collective-permute-start(bf16[64,3584]{1,0:T(8,128)(2,1)S(1)} %shard_map.126), channel_id=1, source_target_pairs={{0,1},{1,2},{2,3},{3,4},{4,5},{5,6},{6,7},{7,8},{8,9},{9,10},{10,1... | collective-permute-start | bytes 1376264 | tf_op jit(solution)/shard_map/ppermute | solution.py:181
  210.7 19.4 %collective-permute-start.48 = (bf16[64,3584]{1,0:T(8,128)(2,1)S(1)}, bf16[64,3584]{1,0:T(8,128)(2,1)S(1)}, u32[]{:S(2)}, u32[]{:S(2)}) collective-permute-start(bf16[64,3584]{1,0:T(8,128)(2,1)S(1)} %shard_map.142), channel_id=1, source_target_pairs={{0,1},{1,2},{2,3},{3,4},{4,5},{5,6},{6,7},{7,8},{8,9},{9,10},{10,1... | collective-permute-start | bytes 1376264 | tf_op jit(solution)/shard_map/ppermute | solution.py:181
  220.6 19.4 %collective-permute-start.33 = (bf16[64,3584]{1,0:T(8,128)(2,1)S(1)}, bf16[64,3584]{1,0:T(8,128)(2,1)S(1)}, u32[]{:S(2)}, u32[]{:S(2)}) collective-permute-start(bf16[64,3584]{1,0:T(8,128)(2,1)S(1)} %shard_map.127), channel_id=1, source_target_pairs={{0,1},{1,2},{2,3},{3,4},{4,5},{5,6},{6,7},{7,8},{8,9},{9,10},{10,1... | collective-permute-start | bytes 1376264 | tf_op jit(solution)/shard_map/ppermute | solution.py:181
  222.8 19.4 %collective-permute-start.56 = (bf16[64,3584]{1,0:T(8,128)(2,1)S(1)}, bf16[64,3584]{1,0:T(8,128)(2,1)S(1)}, u32[]{:S(2)}, u32[]{:S(2)}) collective-permute-start(bf16[64,3584]{1,0:T(8,128)(2,1)S(1)} %shard_map.150), channel_id=1, source_target_pairs={{0,15},{1,0},{2,1},{3,2},{4,3},{5,4},{6,5},{7,6},{8,7},{9,8},{10,9... | collective-permute-start | bytes 1376264 | tf_op jit(solution)/shard_map/ppermute | solution.py:183
  230.4 19.4 %collective-permute-start.49 = (bf16[64,3584]{1,0:T(8,128)(2,1)S(1)}, bf16[64,3584]{1,0:T(8,128)(2,1)S(1)}, u32[]{:S(2)}, u32[]{:S(2)}) collective-permute-start(bf16[64,3584]{1,0:T(8,128)(2,1)S(1)} %shard_map.143), channel_id=1, source_target_pairs={{0,1},{1,2},{2,3},{3,4},{4,5},{5,6},{6,7},{7,8},{8,9},{9,10},{10,1... | collective-permute-start | bytes 1376264 | tf_op jit(solution)/shard_map/ppermute | solution.py:181
  240.2 19.4 %collective-permute-start.34 = (bf16[64,3584]{1,0:T(8,128)(2,1)S(1)}, bf16[64,3584]{1,0:T(8,128)(2,1)S(1)}, u32[]{:S(2)}, u32[]{:S(2)}) collective-permute-start(bf16[64,3584]{1,0:T(8,128)(2,1)S(1)} %shard_map.128), channel_id=1, source_target_pairs={{0,1},{1,2},{2,3},{3,4},{4,5},{5,6},{6,7},{7,8},{8,9},{9,10},{10,1... | collective-permute-start | bytes 1376264 | tf_op jit(solution)/shard_map/ppermute | solution.py:181
  250.1 19.4 %collective-permute-start.50 = (bf16[64,3584]{1,0:T(8,128)(2,1)S(1)}, bf16[64,3584]{1,0:T(8,128)(2,1)S(1)}, u32[]{:S(2)}, u32[]{:S(2)}) collective-permute-start(bf16[64,3584]{1,0:T(8,128)(2,1)S(1)} %shard_map.144), channel_id=1, source_target_pairs={{0,1},{1,2},{2,3},{3,4},{4,5},{5,6},{6,7},{7,8},{8,9},{9,10},{10,1... | collective-permute-start | bytes 1376264 | tf_op jit(solution)/shard_map/ppermute | solution.py:181
  269.7 19.6 %collective-permute-start.51 = (bf16[64,3584]{1,0:T(8,128)(2,1)S(1)}, bf16[64,3584]{1,0:T(8,128)(2,1)S(1)}, u32[]{:S(2)}, u32[]{:S(2)}) collective-permute-start(bf16[64,3584]{1,0:T(8,128)(2,1)S(1)} %shard_map.145), channel_id=1, source_target_pairs={{0,1},{1,2},{2,3},{3,4},{4,5},{5,6},{6,7},{7,8},{8,9},{9,10},{10,1... | collective-permute-start | bytes 1376264 | tf_op jit(solution)/shard_map/ppermute | solution.py:181
  279.5 19.4 %collective-permute-start.36 = (bf16[64,3584]{1,0:T(8,128)(2,1)S(1)}, bf16[64,3584]{1,0:T(8,128)(2,1)S(1)}, u32[]{:S(2)}, u32[]{:S(2)}) collective-permute-start(bf16[64,3584]{1,0:T(8,128)(2,1)S(1)} %shard_map.130), channel_id=1, source_target_pairs={{0,1},{1,2},{2,3},{3,4},{4,5},{5,6},{6,7},{7,8},{8,9},{9,10},{10,1... | collective-permute-start | bytes 1376264 | tf_op jit(solution)/shard_map/ppermute | solution.py:181
  281.8 22.1 %collective-permute-start.59 = (bf16[64,3584]{1,0:T(8,128)(2,1)S(1)}, bf16[64,3584]{1,0:T(8,128)(2,1)S(1)}, u32[]{:S(2)}, u32[]{:S(2)}) collective-permute-start(bf16[64,3584]{1,0:T(8,128)(2,1)S(1)} %shard_map.153), channel_id=1, source_target_pairs={{0,15},{1,0},{2,1},{3,2},{4,3},{5,4},{6,5},{7,6},{8,7},{9,8},{10,9... | collective-permute-start | bytes 1376264 | tf_op jit(solution)/shard_map/ppermute | solution.py:183
  287.4 24.1 %collective-permute-start.44 = (bf16[64,3584]{1,0:T(8,128)(2,1)}, bf16[64,3584]{1,0:T(8,128)(2,1)}, u32[]{:S(2)}, u32[]{:S(2)}) collective-permute-start(bf16[64,3584]{1,0:T(8,128)(2,1)} %shard_map.138), channel_id=1, source_target_pairs={{0,15},{1,0},{2,1},{3,2},{4,3},{5,4},{6,5},{7,6},{8,7},{9,8},{10,9... | collective-permute-start | bytes 1376264 | tf_op jit(solution)/shard_map/ppermute | solution.py:183
  301.9 23.9 %collective-permute-start.52 = (bf16[64,3584]{1,0:T(8,128)(2,1)}, bf16[64,3584]{1,0:T(8,128)(2,1)}, u32[]{:S(2)}, u32[]{:S(2)}) collective-permute-start(bf16[64,3584]{1,0:T(8,128)(2,1)} %shard_map.146), channel_id=1, source_target_pairs={{0,1},{1,2},{2,3},{3,4},{4,5},{5,6},{6,7},{7,8},{8,9},{9,10},{10,1... | collective-permute-start | bytes 1376264 | tf_op jit(solution)/shard_map/ppermute | solution.py:181
  304.9 20.9 %collective-permute-start.60 = (bf16[64,3584]{1,0:T(8,128)(2,1)}, bf16[64,3584]{1,0:T(8,128)(2,1)}, u32[]{:S(2)}, u32[]{:S(2)}) collective-permute-start(bf16[64,3584]{1,0:T(8,128)(2,1)} %shard_map.154), channel_id=1, source_target_pairs={{0,15},{1,0},{2,1},{3,2},{4,3},{5,4},{6,5},{7,6},{8,7},{9,8},{10,9... | collective-permute-start | bytes 1376264 | tf_op jit(solution)/shard_map/ppermute | solution.py:183
  (41 other events, 616.2 us)

commit v2 on v1

--- a/solution.py
+++ b/solution.py
@@ -7,7 +7,9 @@
 
 EXP_SECTION = 2
 TAIL = 128
-VMEM_LIMIT = 48 * 1024 * 1024
+OWN_STEP = 1
+BASE_STEPS = ((3, 4), (5, 6))
+VMEM_LIMIT = 16 * 1024 * 1024
 
 
 def call(kernel, out_shape, flops, moved, **options):
@@ -36,16 +38,15 @@
     return call(kernel, shape, 4 * rows * width, 4 * rows * width)(*operands)
 
 
-def hidden_of(tokens, gate_up):
-    units = gate_up.shape[1] // 2
-    both = jnp.dot(tokens, gate_up, preferred_element_type=jnp.float32)
-    gated, upper = both[:, :units], both[:, units:]
+def hidden_of(tokens, gate, up):
+    gated = jnp.dot(tokens, gate, preferred_element_type=jnp.float32)
+    upper = jnp.dot(tokens, up, preferred_element_type=jnp.float32)
     return gated / (1.0 + jnp.exp(-gated)) * upper
 
 
-def hidden_rows(blocks, carriers, lanes, expert, gate_up):
+def hidden_rows(blocks, carriers, lanes, expert, gate, up):
     count = len(blocks)
-    width, units = gate_up.shape[0], gate_up.shape[1] // 2
+    width, units = gate.shape
     rows = blocks[0].shape[0]
     given = []
     for block in list(blocks) + list(carriers):
@@ -54,10 +55,10 @@
     place = [[block is other for other in given].index(True) for block in blocks]
     bearer = [[block is other for other in given].index(True) for block in carriers]
 
-    def kernel(expert_ref, gate_up_ref, *refs):
+    def kernel(expert_ref, gate_ref, up_ref, *refs):
         mine = expert_ref[0].astype(jnp.float32)
         for i in range(count):
-            hidden = hidden_of(refs[place[i]][:, :width], gate_up_ref[...])
+            hidden = hidden_of(refs[place[i]][:, :width], gate_ref[...], up_ref[...])
             picks = refs[bearer[i]][:, lanes[i] : lanes[i] + 1].astype(jnp.float32)
             refs[len(given) + i][...] = jnp.where(picks == mine, hidden, 0.0).astype(
                 jnp.bfloat16
@@ -71,8 +72,8 @@
         shape,
         flops,
         4 * width * units + 2 * count * rows * width,
-        in_specs=[pl.BlockSpec(memory_space=pltpu.SMEM)] + [vmem] * (1 + len(given)),
-    )(expert, gate_up, *given)
+        in_specs=[pl.BlockSpec(memory_space=pltpu.SMEM)] + [vmem] * (2 + len(given)),
+    )(expert, gate, up, *given)
 
 
 def add_partial(hidden, down, arrived):
@@ -91,18 +92,47 @@
     )
 
 
-def finish(hidden, down, arrived, inputs, weights_in):
-    def kernel(hidden_ref, down_ref, a_ref, b_ref, inputs_ref, weights_ref, out_ref):
-        total = jnp.dot(hidden_ref[...], down_ref[...], preferred_element_type=jnp.float32)
-        total = total + a_ref[...].astype(jnp.float32) + b_ref[...].astype(jnp.float32)
-        moved = inputs_ref[...].astype(jnp.float32) + weights_ref[...] * total
-        out_ref[...] = moved.astype(jnp.bfloat16)
-
+def residual(hidden, down, inputs, weights_in):
     rows, width = inputs.shape
-    shape = jax.ShapeDtypeStruct((rows, width), jnp.bfloat16)
+
+    def kernel(hidden_ref, down_ref, inputs_ref, weights_ref, high_ref, low_ref):
+        own = jnp.dot(hidden_ref[...], down_ref[...], preferred_element_type=jnp.float32)
+        total = inputs_ref[...].astype(jnp.float32) + weights_ref[...] * own
+        high = total.astype(jnp.bfloat16)
+        high_ref[:, :width] = high
+        low_ref[...] = (total - high.astype(jnp.float32)).astype(jnp.bfloat16)
+        lane = lax.broadcasted_iota(jnp.int32, (rows, TAIL), 1)
+        rest = jnp.broadcast_to(weights_ref[...], (rows, TAIL))
+        columns = jnp.zeros((rows, TAIL), jnp.float32)
+        for part in range(3):
+            piece = rest.astype(jnp.bfloat16).astype(jnp.float32)
+            columns = jnp.where(lane == part, piece, columns)
+            rest = rest - piece
+        high_ref[:, width:] = columns.astype(jnp.bfloat16)
+
+    shape = [
+        jax.ShapeDtypeStruct((rows, width + TAIL), jnp.bfloat16),
+        jax.ShapeDtypeStruct((rows, width), jnp.bfloat16),
+    ]
     return call(kernel, shape, 2 * rows * hidden.shape[1] * width, 8 * rows * width)(
-        hidden, down, *arrived, inputs, weights_in
-    )
+        hidden, down, inputs, weights_in
+    )
+
+
+def finish(base, arrived):
+    high, low = base
+    rows, width = low.shape
+
+    def kernel(high_ref, low_ref, a_ref, b_ref, out_ref):
+        weight = jnp.sum(
+            high_ref[:, width:].astype(jnp.float32), axis=1, keepdims=True
+        )
+        total = a_ref[...].astype(jnp.float32) + b_ref[...].astype(jnp.float32)
+        moved = high_ref[:, :width].astype(jnp.float32) + low_ref[...].astype(jnp.float32)
+        out_ref[0] = (moved + weight * total).astype(jnp.bfloat16)
+
+    shape = jax.ShapeDtypeStruct((1, rows, width), jnp.bfloat16)
+    return call(kernel, shape, 4 * rows * width, 10 * rows * width)(high, low, *arrived)
 
 
 def per_device(
@@ -117,8 +147,7 @@
     up_weight,
     down_weight,
 ):
-    down = down_weight[0]
-    gate_up = jnp.concatenate([gate_weight[0], up_weight[0]], axis=1)
+    gate, up, down = gate_weight[0], up_weight[0], down_weight[0]
     acts_down, acts_up = inputs_down[0], inputs_up[0]
     rows, width = acts_down.shape
     ring = lax.axis_size("expert")
@@ -136,9 +165,6 @@
     normed = (norm_rows(acts_down, norm_gain, tail), norm_rows(acts_up, norm_gain))
 
     hidden = [{}, {}]
-    hidden[0][0], hidden[1][0] = hidden_rows(
-        normed, (normed[0], normed[0]), lanes, expert, gate_up
-    )
     ahead, behind = list(normed), list(normed)
     for step in range(1, half + 1):
         for way in range(2):
@@ -153,6 +179,24 @@
                 behind[way], hidden[way][1 - step] = lax.optimization_barrier(
                     (behind[way], hidden[way][1 - step])
                 )
+            if step in BASE_STEPS[way]:
+                part = BASE_STEPS[way].index(step)
+                ahead[way], base[way][part] = lax.optimization_barrier(
+                    (ahead[way], base[way][part])
+                )
+        if step == OWN_STEP:
+            behind[0], *mine = lax.optimization_barrier((behind[0], *normed))
+            hidden[0][0], hidden[1][0] = hidden_rows(
+                mine, (mine[0], mine[0]), lanes, expert, gate, up
+            )
+            sections = lax.axis_size("section")
+            base = [None, None]
+            for way, acts, probs in ((0, acts_down, probs_down[0]), (1, acts_up, probs_up[0])):
+                route = [(i, (i + 1 - 2 * way) % sections) for i in range(sections)]
+                base[way] = [
+                    lax.ppermute(part, "section", route)
+                    for part in residual(hidden[way][0], down, acts, probs)
+                ]
         if step < half:
             (
                 hidden[0][step],
@@ -164,38 +208,41 @@
                 (ahead[0], ahead[0], behind[0], behind[0]),
                 lanes * 2,
                 expert,
-                gate_up,
+                gate,
+                up,
             )
         else:
             hidden[0][half], hidden[1][-half] = hidden_rows(
-                (ahead[0], behind[1]), (ahead[0], ahead[0]), lanes, expert, gate_up
+                (ahead[0], behind[1]), (ahead[0], ahead[0]), lanes, expert, gate, up
             )
 
     def add(way, offset, arrived):
         return add_partial(hidden[way][offset], down, arrived)
+
+    def last_hop(value, way, shift):
+        route = [
+            (i * ring + j, (i + 1 - 2 * way) % sections * ring + (j + shift) % ring)
+            for i in range(sections)
+            for j in range(ring)
+        ]
+        return lax.ppermute(value, ("section", "expert"), route)
 
     onward, returning = [None, None], [None, None]
     for step in range(half, 0, -1):
         for way in range(2):
             if step < half or way == 0:
-                onward[way] = lax.ppermute(add(way, step, onward[way]), "expert", forward)
+                onward[way] = add(way, step, onward[way])
+                if step > 1:
+                    onward[way] = lax.ppermute(onward[way], "expert", forward)
+                else:
+                    onward[way] = last_hop(onward[way], way, 1)
             if step < half or way == 1:
-                returning[way] = lax.ppermute(
-                    add(way, -step, returning[way]), "expert", backward
-                )
-    moved_down, moved_up = (
-        finish(hidden[way][0], down, (onward[way], returning[way]), acts, probs)
-        for way, acts, probs in ((0, acts_down, probs_down[0]), (1, acts_up, probs_up[0]))
-    )
-
-    sections = lax.axis_size("section")
-    next_down = lax.ppermute(
-        moved_down, "section", [(i, (i + 1) % sections) for i in range(sections)]
-    )
-    next_up = lax.ppermute(
-        moved_up, "section", [(i, (i - 1) % sections) for i in range(sections)]
-    )
-    return (next_down[None], next_up[None])
+                returning[way] = add(way, -step, returning[way])
+                if step > 1:
+                    returning[way] = lax.ppermute(returning[way], "expert", backward)
+                else:
+                    returning[way] = last_hop(returning[way], way, -1)
+    return tuple(finish(base[way], (onward[way], returning[way])) for way in range(2))
 
 
 def solution(mesh):

time: 342 us -> 332 us (0.971)
  waiting for transfers between devices: 91.9 us -> 70.9 us
  starting transfers between devices: 209 us -> 222 us
    ppermute x32 -> x34, starting transfers between devices: 100 us -> 116 us  [the longest x13 50.6 us: per_device(): returning[way] = lax.ppermute(returning[way], 'expert', backward)]
    ppermute x15, waiting for transfers between devices: 14.2 us -> 1.09 us  [per_device(): ahead[way] = lax.ppermute(ahead[way], 'expert', backward)]
    ppermute x32 -> x34, waiting for transfers between devices: 53.5 us -> 46.6 us  [the longest x13 34.8 us: per_device(): onward[way] = lax.ppermute(onward[way], 'expert', forward)]
    pallas_call x9, Pallas kernels: 12.6 us -> 17.2 us  [hidden_rows(): call(kernel, shape, flops, 4 * width * units + 2 * count * rows * width,...]
  transfers between devices with their start and end apart: 62 -> 64, of which waited for: 38 -> 17; matrix products, arithmetic and copies ran while one was open for 1% -> 0% of each run, Pallas kernels for 8% -> 8%
where the time goes in v2:
time: 332 us; the launch traced here: 330 us
  starting transfers between devices  222 us (67%)
  waiting for transfers between devices  70.9 us (21%)
  Pallas kernels  29 us (9%)
  local copies, waits for them, and re-layouts  5.4 us (2%)
    ppermute x15, starting transfers between devices, per_device(): ahead[way] = lax.ppermute(ahead[way], 'expert', backward)  77 us
    ppermute x13, starting transfers between devices, per_device(): returning[way] = lax.ppermute(returning[way], 'expert', backward)  50.6 us
    ppermute x13, waiting for transfers between devices, per_device(): onward[way] = lax.ppermute(onward[way], 'expert', forward)  34.8 us
    ppermute x15, starting transfers between devices, per_device(): behind[way] = lax.ppermute(behind[way], 'expert', forward)  29.1 us
    ppermute x13, starting transfers between devices, per_device(): onward[way] = lax.ppermute(onward[way], 'expert', forward)  27.4 us
    ppermute x15, waiting for transfers between devices, per_device(): behind[way] = lax.ppermute(behind[way], 'expert', forward)  23.2 us
    ppermute x4, starting transfers between devices, last_hop(): return lax.ppermute(value, ('section', 'expert'), route)  20.8 us
    pallas_call x9, Pallas kernels, hidden_rows(): call(kernel, shape, flops, 4 * width * units + 2 * count * rows * width,...  17.2 us
  transfers between devices with their start and end apart: 64, of which 17 were waited for; matrix products, arithmetic and copies ran while one was open for 0% of the time, Pallas kernels for 8%

profile of v2, /device:TPU:1, one launch (start us, length us, event | category | flops | bytes accessed | tf_op | source)
XLA Modules:
  0.0 329.6 jit_solution(7749279696226942883)
XLA Ops:
  3.5 12.1 %collective-permute-start = (bf16[64,3712]{1,0:T(8,128)(2,1)S(1)}, bf16[64,3712]{1,0:T(8,128)(2,1)}, u32[]{:S(2)}, u32[]{:S(2)}) collective-permute-start(bf16[64,3712]{1,0:T(8,128)(2,1)S(1)} %shard_map.113.refs_0_), channel_id=1, source_target_pairs={{0,15},{1,0},{2,1},{3,2},{4,3},{5,4},{6,5},{7,6},{8,7},{9,8},{10,9... | collective-permute-start | bytes 1425416 | tf_op jit(solution)/shard_map/ppermute | solution.py:172
  20.7 4.6 %collective-permute-start.2 = (bf16[64,3584]{1,0:T(8,128)(2,1)S(1)}, bf16[64,3584]{1,0:T(8,128)(2,1)}, u32[]{:S(2)}, u32[]{:S(2)}) collective-permute-start(bf16[64,3584]{1,0:T(8,128)(2,1)S(1)} %shard_map.114.refs_1_), channel_id=1, source_target_pairs={{0,15},{1,0},{2,1},{3,2},{4,3},{5,4},{6,5},{7,6},{8,7},{9,8},{10,9... | collective-permute-start | bytes 1376264 | tf_op jit(solution)/shard_map/ppermute | solution.py:172
  34.9 5.4 %collective-permute-start.6 = (bf16[64,3584]{1,0:T(8,128)(2,1)}, bf16[64,3584]{1,0:T(8,128)(2,1)S(1)}, u32[]{:S(2)}, u32[]{:S(2)}) collective-permute-start(bf16[64,3584]{1,0:T(8,128)(2,1)} %collective-permute-done.2.refs_1_), channel_id=1, source_target_pairs={{0,15},{1,0},{2,1},{3,2},{4,3},{5,4},{6,5},{7,6},{8,7},{9,8},{10,9... | collective-permute-start | bytes 1376264 | tf_op jit(solution)/shard_map/ppermute | solution.py:172
  46.8 4.6 %collective-permute-start.5 = (bf16[64,3712]{1,0:T(8,128)(2,1)}, bf16[64,3712]{1,0:T(8,128)(2,1)S(1)}, u32[]{:S(2)}, u32[]{:S(2)}) collective-permute-start(bf16[64,3712]{1,0:T(8,128)(2,1)} %collective-permute-done.1.refs_0_), channel_id=1, source_target_pairs={{0,15},{1,0},{2,1},{3,2},{4,3},{5,4},{6,5},{7,6},{8,7},{9,8},{10,9... | collective-permute-start | bytes 1425416 | tf_op jit(solution)/shard_map/ppermute | solution.py:172
  51.8 6.9 %collective-permute-start.9 = (bf16[64,3712]{1,0:T(8,128)(2,1)S(1)}, bf16[64,3712]{1,0:T(8,128)(2,1)S(1)}, u32[]{:S(2)}, u32[]{:S(2)}) collective-permute-start(bf16[64,3712]{1,0:T(8,128)(2,1)S(1)} %get-tuple-element.111), channel_id=1, source_target_pairs={{0,16},{16,32},{32,48},{48,64},{64,80},{80,96},{96,112},{112,128},... | collective-permute-start | bytes 1425416 | tf_op jit(solution)/shard_map/ppermute | solution.py:197
  60.6 4.6 %collective-permute-start.11 = (bf16[64,3584]{1,0:T(8,128)(2,1)S(1)}, bf16[64,3584]{1,0:T(8,128)(2,1)}, u32[]{:S(2)}, u32[]{:S(2)}) collective-permute-start(bf16[64,3584]{1,0:T(8,128)(2,1)S(1)} %collective-permute-done.6.refs_1_), channel_id=1, source_target_pairs={{0,15},{1,0},{2,1},{3,2},{4,3},{5,4},{6,5},{7,6},{8,7},{9,8},{10,9... | collective-permute-start | bytes 1376264 | tf_op jit(solution)/shard_map/ppermute | solution.py:172
  69.7 4.6 %collective-permute-start.10 = (bf16[64,3712]{1,0:T(8,128)(2,1)S(1)}, bf16[64,3712]{1,0:T(8,128)(2,1)}, u32[]{:S(2)}, u32[]{:S(2)}) collective-permute-start(bf16[64,3712]{1,0:T(8,128)(2,1)S(1)} %collective-permute-done.5.refs_0_), channel_id=1, source_target_pairs={{0,15},{1,0},{2,1},{3,2},{4,3},{5,4},{6,5},{7,6},{8,7},{9,8},{10,9... | collective-permute-start | bytes 1425416 | tf_op jit(solution)/shard_map/ppermute | solution.py:172
  79.2 4.6 %collective-permute-start.16 = (bf16[64,3584]{1,0:T(8,128)(2,1)}, bf16[64,3584]{1,0:T(8,128)(2,1)}, u32[]{:S(2)}, u32[]{:S(2)}) collective-permute-start(bf16[64,3584]{1,0:T(8,128)(2,1)} %collective-permute-done.11.refs_1_), channel_id=1, source_target_pairs={{0,15},{1,0},{2,1},{3,2},{4,3},{5,4},{6,5},{7,6},{8,7},{9,8},{10,9... | collective-permute-start | bytes 1376264 | tf_op jit(solution)/shard_map/ppermute | solution.py:172
  90.1 4.6 %collective-permute-start.15 = (bf16[64,3712]{1,0:T(8,128)(2,1)}, bf16[64,3712]{1,0:T(8,128)(2,1)}, u32[]{:S(2)}, u32[]{:S(2)}) collective-permute-start(bf16[64,3712]{1,0:T(8,128)(2,1)} %collective-permute-done.10.refs_0_), channel_id=1, source_target_pairs={{0,15},{1,0},{2,1},{3,2},{4,3},{5,4},{6,5},{7,6},{8,7},{9,8},{10,9... | collective-permute-start | bytes 1425416 | tf_op jit(solution)/shard_map/ppermute | solution.py:172
  99.0 4.6 %collective-permute-start.20 = (bf16[64,3584]{1,0:T(8,128)(2,1)}, bf16[64,3584]{1,0:T(8,128)(2,1)S(1)}, u32[]{:S(2)}, u32[]{:S(2)}) collective-permute-start(bf16[64,3584]{1,0:T(8,128)(2,1)} %collective-permute-done.16.refs_1_), channel_id=1, source_target_pairs={{0,15},{1,0},{2,1},{3,2},{4,3},{5,4},{6,5},{7,6},{8,7},{9,8},{10,9... | collective-permute-start | bytes 1376264 | tf_op jit(solution)/shard_map/ppermute | solution.py:172
  109.4 4.6 %collective-permute-start.19 = (bf16[64,3712]{1,0:T(8,128)(2,1)}, bf16[64,3712]{1,0:T(8,128)(2,1)S(1)}, u32[]{:S(2)}, u32[]{:S(2)}) collective-permute-start(bf16[64,3712]{1,0:T(8,128)(2,1)} %collective-permute-done.15.refs_0_), channel_id=1, source_target_pairs={{0,15},{1,0},{2,1},{3,2},{4,3},{5,4},{6,5},{7,6},{8,7},{9,8},{10,9... | collective-permute-start | bytes 1425416 | tf_op jit(solution)/shard_map/ppermute | solution.py:172
  116.0 4.9 %collective-permute-start.26 = (bf16[64,3584]{1,0:T(8,128)(2,1)S(1)}, bf16[64,3584]{1,0:T(8,128)(2,1)S(1)}, u32[]{:S(2)}, u32[]{:S(2)}) collective-permute-start(bf16[64,3584]{1,0:T(8,128)(2,1)S(1)} %get-tuple-element.151), channel_id=1, source_target_pairs={{0,496},{16,0},{32,16},{48,32},{64,48},{80,64},{96,80},{112,96},{1... | collective-permute-start | bytes 1376264 | tf_op jit(solution)/shard_map/ppermute | solution.py:197
  120.9 4.9 %collective-permute-start.25 = (bf16[64,3584]{1,0:T(8,128)(2,1)S(1)}, bf16[64,3584]{1,0:T(8,128)(2,1)S(1)}, u32[]{:S(2)}, u32[]{:S(2)}) collective-permute-start(bf16[64,3584]{1,0:T(8,128)(2,1)S(1)} %collective-permute-done.20.refs_1_), channel_id=1, source_target_pairs={{0,15},{1,0},{2,1},{3,2},{4,3},{5,4},{6,5},{7,6},{8,7},{9,8},{10,9... | collective-permute-start | bytes 1376264 | tf_op jit(solution)/shard_map/ppermute | solution.py:172
  130.2 4.6 %collective-permute-start.24 = (bf16[64,3712]{1,0:T(8,128)(2,1)S(1)}, bf16[64,3712]{1,0:T(8,128)(2,1)S(1)}, u32[]{:S(2)}, u32[]{:S(2)}) collective-permute-start(bf16[64,3712]{1,0:T(8,128)(2,1)S(1)} %collective-permute-done.19.refs_0_), channel_id=1, source_target_pairs={{0,15},{1,0},{2,1},{3,2},{4,3},{5,4},{6,5},{7,6},{8,7},{9,8},{10,9... | collective-permute-start | bytes 1425416 | tf_op jit(solution)/shard_map/ppermute | solution.py:172
  136.9 7.0 %collective-permute-done.27.refs_2_ = bf16[64,3712]{1,0:T(8,128)(2,1)S(1)} collective-permute-done((bf16[64,3712]{1,0:T(8,128)(2,1)S(1)}, bf16[64,3712]{1,0:T(8,128)(2,1)S(1)}, u32[]{:S(2)}, u32[]{:S(2)}) %collective-permute-start.27) | collective-permute-done | bytes 475168 | tf_op jit(solution)/shard_map/ppermute | solution.py:174
  157.6 4.6 %collective-permute-start.29 = (bf16[64,3584]{1,0:T(8,128)(2,1)S(1)}, bf16[64,3584]{1,0:T(8,128)(2,1)S(1)}, u32[]{:S(2)}, u32[]{:S(2)}) collective-permute-start(bf16[64,3584]{1,0:T(8,128)(2,1)S(1)} %collective-permute-done.25.refs_1_), channel_id=1, source_target_pairs={{0,15},{1,0},{2,1},{3,2},{4,3},{5,4},{6,5},{7,6},{8,7},{9,8},{10,9... | collective-permute-start | bytes 1376264 | tf_op jit(solution)/shard_map/ppermute | solution.py:172
  162.2 6.2 %collective-permute-done.33.refs_1_ = bf16[64,3584]{1,0:T(8,128)(2,1)S(1)} collective-permute-done((bf16[64,3584]{1,0:T(8,128)(2,1)S(1)}, bf16[64,3584]{1,0:T(8,128)(2,1)S(1)}, u32[]{:S(2)}, u32[]{:S(2)}) %collective-permute-start.33) | collective-permute-done | bytes 458784 | tf_op jit(solution)/shard_map/ppermute | solution.py:174
  171.6 4.6 %collective-permute-start.56 = (bf16[64,3584]{1,0:T(8,128)(2,1)S(1)}, bf16[64,3584]{1,0:T(8,128)(2,1)S(1)}, u32[]{:S(2)}, u32[]{:S(2)}) collective-permute-start(bf16[64,3584]{1,0:T(8,128)(2,1)S(1)} %shard_map.149), channel_id=1, source_target_pairs={{0,15},{1,0},{2,1},{3,2},{4,3},{5,4},{6,5},{7,6},{8,7},{9,8},{10,9... | collective-permute-start | bytes 1376264 | tf_op jit(solution)/shard_map/ppermute | solution.py:242
  190.9 4.6 %collective-permute-start.57 = (bf16[64,3584]{1,0:T(8,128)(2,1)S(1)}, bf16[64,3584]{1,0:T(8,128)(2,1)S(1)}, u32[]{:S(2)}, u32[]{:S(2)}) collective-permute-start(bf16[64,3584]{1,0:T(8,128)(2,1)S(1)} %shard_map.150), channel_id=1, source_target_pairs={{0,15},{1,0},{2,1},{3,2},{4,3},{5,4},{6,5},{7,6},{8,7},{9,8},{10,9... | collective-permute-start | bytes 1376264 | tf_op jit(solution)/shard_map/ppermute | solution.py:242
  201.3 6.0 %collective-permute-done.35.refs_0_ = bf16[64,3584]{1,0:T(8,128)(2,1)S(1)} collective-permute-done((bf16[64,3584]{1,0:T(8,128)(2,1)S(1)}, bf16[64,3584]{1,0:T(8,128)(2,1)S(1)}, u32[]{:S(2)}, u32[]{:S(2)}) %collective-permute-start.35) | collective-permute-done | bytes 458784 | tf_op jit(solution)/shard_map/ppermute | solution.py:236
  209.8 4.6 %collective-permute-start.58 = (bf16[64,3584]{1,0:T(8,128)(2,1)S(1)}, bf16[64,3584]{1,0:T(8,128)(2,1)S(1)}, u32[]{:S(2)}, u32[]{:S(2)}) collective-permute-start(bf16[64,3584]{1,0:T(8,128)(2,1)S(1)} %shard_map.151), channel_id=1, source_target_pairs={{0,15},{1,0},{2,1},{3,2},{4,3},{5,4},{6,5},{7,6},{8,7},{9,8},{10,9... | collective-permute-start | bytes 1376264 | tf_op jit(solution)/shard_map/ppermute | solution.py:242
  220.9 6.1 %collective-permute-done.36.refs_0_ = bf16[64,3584]{1,0:T(8,128)(2,1)S(1)} collective-permute-done((bf16[64,3584]{1,0:T(8,128)(2,1)S(1)}, bf16[64,3584]{1,0:T(8,128)(2,1)S(1)}, u32[]{:S(2)}, u32[]{:S(2)}) %collective-permute-start.36) | collective-permute-done | bytes 458784 | tf_op jit(solution)/shard_map/ppermute | solution.py:236
  229.5 4.6 %collective-permute-start.59 = (bf16[64,3584]{1,0:T(8,128)(2,1)S(1)}, bf16[64,3584]{1,0:T(8,128)(2,1)S(1)}, u32[]{:S(2)}, u32[]{:S(2)}) collective-permute-start(bf16[64,3584]{1,0:T(8,128)(2,1)S(1)} %shard_map.152), channel_id=1, source_target_pairs={{0,15},{1,0},{2,1},{3,2},{4,3},{5,4},{6,5},{7,6},{8,7},{9,8},{10,9... | collective-permute-start | bytes 1376264 | tf_op jit(solution)/shard_map/ppermute | solution.py:242
  239.9 6.7 %collective-permute-done.37.refs_0_ = bf16[64,3584]{1,0:T(8,128)(2,1)S(1)} collective-permute-done((bf16[64,3584]{1,0:T(8,128)(2,1)S(1)}, bf16[64,3584]{1,0:T(8,128)(2,1)S(1)}, u32[]{:S(2)}, u32[]{:S(2)}) %collective-permute-start.37) | collective-permute-done | bytes 458784 | tf_op jit(solution)/shard_map/ppermute | solution.py:236
  249.1 4.6 %collective-permute-start.60 = (bf16[64,3584]{1,0:T(8,128)(2,1)S(1)}, bf16[64,3584]{1,0:T(8,128)(2,1)S(1)}, u32[]{:S(2)}, u32[]{:S(2)}) collective-permute-start(bf16[64,3584]{1,0:T(8,128)(2,1)S(1)} %shard_map.153), channel_id=1, source_target_pairs={{0,15},{1,0},{2,1},{3,2},{4,3},{5,4},{6,5},{7,6},{8,7},{9,8},{10,9... | collective-permute-start | bytes 1376264 | tf_op jit(solution)/shard_map/ppermute | solution.py:242
  259.6 6.7 %collective-permute-done.38.refs_0_ = bf16[64,3584]{1,0:T(8,128)(2,1)S(1)} collective-permute-done((bf16[64,3584]{1,0:T(8,128)(2,1)S(1)}, bf16[64,3584]{1,0:T(8,128)(2,1)S(1)}, u32[]{:S(2)}, u32[]{:S(2)}) %collective-permute-start.38) | collective-permute-done | bytes 458784 | tf_op jit(solution)/shard_map/ppermute | solution.py:236
  268.8 4.6 %collective-permute-start.61 = (bf16[64,3584]{1,0:T(8,128)(2,1)S(1)}, bf16[64,3584]{1,0:T(8,128)(2,1)S(1)}, u32[]{:S(2)}, u32[]{:S(2)}) collective-permute-start(bf16[64,3584]{1,0:T(8,128)(2,1)S(1)} %shard_map.154), channel_id=1, source_target_pairs={{0,15},{1,0},{2,1},{3,2},{4,3},{5,4},{6,5},{7,6},{8,7},{9,8},{10,9... | collective-permute-start | bytes 1376264 | tf_op jit(solution)/shard_map/ppermute | solution.py:242
  279.2 6.7 %collective-permute-done.39.refs_0_ = bf16[64,3584]{1,0:T(8,128)(2,1)S(1)} collective-permute-done((bf16[64,3584]{1,0:T(8,128)(2,1)S(1)}, bf16[64,3584]{1,0:T(8,128)(2,1)S(1)}, u32[]{:S(2)}, u32[]{:S(2)}) %collective-permute-start.39) | collective-permute-done | bytes 458784 | tf_op jit(solution)/shard_map/ppermute | solution.py:236
  288.7 4.6 %collective-permute-start.62 = (bf16[64,3584]{1,0:T(8,128)(2,1)S(1)}, bf16[64,3584]{1,0:T(8,128)(2,1)S(1)}, u32[]{:S(2)}, u32[]{:S(2)}) collective-permute-start(bf16[64,3584]{1,0:T(8,128)(2,1)S(1)} %shard_map.155), channel_id=1, source_target_pairs={{0,15},{1,0},{2,1},{3,2},{4,3},{5,4},{6,5},{7,6},{8,7},{9,8},{10,9... | collective-permute-start | bytes 1376264 | tf_op jit(solution)/shard_map/ppermute | solution.py:242
  293.5 9.9 %collective-permute-start.48 = (bf16[64,3584]{1,0:T(8,128)(2,1)S(1)}, bf16[64,3584]{1,0:T(8,128)(2,1)S(1)}, u32[]{:S(2)}, u32[]{:S(2)}) collective-permute-start(bf16[64,3584]{1,0:T(8,128)(2,1)S(1)} %shard_map.140), channel_id=1, source_target_pairs={{0,31},{1,16},{2,17},{3,18},{4,19},{5,20},{6,21},{7,22},{8,23},{9,... | collective-permute-start | bytes 1376264 | tf_op jit(solution)/shard_map/ppermute | solution.py:228
  310.6 4.7 %collective-permute-start.63 = (bf16[64,3584]{1,0:T(8,128)(2,1)S(1)}, bf16[64,3584]{1,0:T(8,128)(2,1)S(1)}, u32[]{:S(2)}, u32[]{:S(2)}) collective-permute-start(bf16[64,3584]{1,0:T(8,128)(2,1)S(1)} %shard_map.156), channel_id=1, source_target_pairs={{0,511},{1,496},{2,497},{3,498},{4,499},{5,500},{6,501},{7,502},{8... | collective-permute-start | bytes 1376264 | tf_op jit(solution)/shard_map/ppermute | solution.py:228
  315.3 11.7 %collective-permute-done.41.a_ref = bf16[64,3584]{1,0:T(8,128)(2,1)S(1)} collective-permute-done((bf16[64,3584]{1,0:T(8,128)(2,1)S(1)}, bf16[64,3584]{1,0:T(8,128)(2,1)S(1)}, u32[]{:S(2)}, u32[]{:S(2)}) %collective-permute-start.41) | collective-permute-done | bytes 458784 | tf_op jit(solution)/shard_map/ppermute | solution.py:228
  (180 shorter events, 144.1 us)
Async XLA Ops:
  3.5 22.5 %collective-permute-start = (bf16[64,3712]{1,0:T(8,128)(2,1)S(1)}, bf16[64,3712]{1,0:T(8,128)(2,1)}, u32[]{:S(2)}, u32[]{:S(2)}) collective-permute-start(bf16[64,3712]{1,0:T(8,128)(2,1)S(1)} %shard_map.113.refs_0_), channel_id=1, source_target_pairs={{0,15},{1,0},{2,1},{3,2},{4,3},{5,4},{6,5},{7,6},{8,7},{9,8},{10,9... | collective-permute-start | bytes 1425416 | tf_op jit(solution)/shard_map/ppermute | solution.py:172
  18.8 22.5 %collective-permute-start.3 = (bf16[64,3712]{1,0:T(8,128)(2,1)S(1)}, bf16[64,3712]{1,0:T(8,128)(2,1)}, u32[]{:S(2)}, u32[]{:S(2)}) collective-permute-start(bf16[64,3712]{1,0:T(8,128)(2,1)S(1)} %shard_map.113.refs_0_), channel_id=1, source_target_pairs={{0,1},{1,2},{2,3},{3,4},{4,5},{5,6},{6,7},{7,8},{8,9},{9,10},{10,1... | collective-permute-start | bytes 1425416 | tf_op jit(solution)/shard_map/ppermute | solution.py:174
  26.1 20.7 %collective-permute-start.1 = (bf16[64,3712]{1,0:T(8,128)(2,1)}, bf16[64,3712]{1,0:T(8,128)(2,1)}, u32[]{:S(2)}, u32[]{:S(2)}) collective-permute-start(bf16[64,3712]{1,0:T(8,128)(2,1)} %collective-permute-done.refs_0_), channel_id=1, source_target_pairs={{0,15},{1,0},{2,1},{3,2},{4,3},{5,4},{6,5},{7,6},{8,7},{9,8},{10,9... | collective-permute-start | bytes 1425416 | tf_op jit(solution)/shard_map/ppermute | solution.py:172
  31.1 27.5 %collective-permute-start.8 = (bf16[64,3584]{1,0:T(8,128)(2,1)}, bf16[64,3584]{1,0:T(8,128)(2,1)}, u32[]{:S(2)}, u32[]{:S(2)}) collective-permute-start(bf16[64,3584]{1,0:T(8,128)(2,1)} %collective-permute-done.4.refs_3_), channel_id=1, source_target_pairs={{0,1},{1,2},{2,3},{3,4},{4,5},{5,6},{6,7},{7,8},{8,9},{9,10},{10,1... | collective-permute-start | bytes 1376264 | tf_op jit(solution)/shard_map/ppermute | solution.py:174
  34.9 25.7 %collective-permute-start.6 = (bf16[64,3584]{1,0:T(8,128)(2,1)}, bf16[64,3584]{1,0:T(8,128)(2,1)S(1)}, u32[]{:S(2)}, u32[]{:S(2)}) collective-permute-start(bf16[64,3584]{1,0:T(8,128)(2,1)} %collective-permute-done.2.refs_1_), channel_id=1, source_target_pairs={{0,15},{1,0},{2,1},{3,2},{4,3},{5,4},{6,5},{7,6},{8,7},{9,8},{10,9... | collective-permute-start | bytes 1376264 | tf_op jit(solution)/shard_map/ppermute | solution.py:172
  41.3 23.9 %collective-permute-start.7 = (bf16[64,3712]{1,0:T(8,128)(2,1)}, bf16[64,3712]{1,0:T(8,128)(2,1)S(1)}, u32[]{:S(2)}, u32[]{:S(2)}) collective-permute-start(bf16[64,3712]{1,0:T(8,128)(2,1)} %collective-permute-done.3.refs_2_), channel_id=1, source_target_pairs={{0,1},{1,2},{2,3},{3,4},{4,5},{5,6},{6,7},{7,8},{8,9},{9,10},{10,1... | collective-permute-start | bytes 1425416 | tf_op jit(solution)/shard_map/ppermute | solution.py:174
  46.8 22.9 %collective-permute-start.5 = (bf16[64,3712]{1,0:T(8,128)(2,1)}, bf16[64,3712]{1,0:T(8,128)(2,1)S(1)}, u32[]{:S(2)}, u32[]{:S(2)}) collective-permute-start(bf16[64,3712]{1,0:T(8,128)(2,1)} %collective-permute-done.1.refs_0_), channel_id=1, source_target_pairs={{0,15},{1,0},{2,1},{3,2},{4,3},{5,4},{6,5},{7,6},{8,7},{9,8},{10,9... | collective-permute-start | bytes 1425416 | tf_op jit(solution)/shard_map/ppermute | solution.py:172
  65.2 19.6 %collective-permute-start.12 = (bf16[64,3712]{1,0:T(8,128)(2,1)S(1)}, bf16[64,3712]{1,0:T(8,128)(2,1)}, u32[]{:S(2)}, u32[]{:S(2)}) collective-permute-start(bf16[64,3712]{1,0:T(8,128)(2,1)S(1)} %collective-permute-done.7.refs_2_), channel_id=1, source_target_pairs={{0,1},{1,2},{2,3},{3,4},{4,5},{5,6},{6,7},{7,8},{8,9},{9,10},{10,1... | collective-permute-start | bytes 1425416 | tf_op jit(solution)/shard_map/ppermute | solution.py:174
  69.7 19.7 %collective-permute-start.10 = (bf16[64,3712]{1,0:T(8,128)(2,1)S(1)}, bf16[64,3712]{1,0:T(8,128)(2,1)}, u32[]{:S(2)}, u32[]{:S(2)}) collective-permute-start(bf16[64,3712]{1,0:T(8,128)(2,1)S(1)} %collective-permute-done.5.refs_0_), channel_id=1, source_target_pairs={{0,15},{1,0},{2,1},{3,2},{4,3},{5,4},{6,5},{7,6},{8,7},{9,8},{10,9... | collective-permute-start | bytes 1425416 | tf_op jit(solution)/shard_map/ppermute | solution.py:172
  79.2 19.8 %collective-permute-start.16 = (bf16[64,3584]{1,0:T(8,128)(2,1)}, bf16[64,3584]{1,0:T(8,128)(2,1)}, u32[]{:S(2)}, u32[]{:S(2)}) collective-permute-start(bf16[64,3584]{1,0:T(8,128)(2,1)} %collective-permute-done.11.refs_1_), channel_id=1, source_target_pairs={{0,15},{1,0},{2,1},{3,2},{4,3},{5,4},{6,5},{7,6},{8,7},{9,8},{10,9... | collective-permute-start | bytes 1376264 | tf_op jit(solution)/shard_map/ppermute | solution.py:172
  84.7 20.0 %collective-permute-start.17 = (bf16[64,3712]{1,0:T(8,128)(2,1)}, bf16[64,3712]{1,0:T(8,128)(2,1)}, u32[]{:S(2)}, u32[]{:S(2)}) collective-permute-start(bf16[64,3712]{1,0:T(8,128)(2,1)} %collective-permute-done.12.refs_2_), channel_id=1, source_target_pairs={{0,1},{1,2},{2,3},{3,4},{4,5},{5,6},{6,7},{7,8},{8,9},{9,10},{10,1... | collective-permute-start | bytes 1425416 | tf_op jit(solution)/shard_map/ppermute | solution.py:174
  97.1 23.8 %collective-permute-start.21 = (bf16[64,3712]{1,0:T(8,128)(2,1)S(1)}, bf16[64,3712]{1,0:T(8,128)(2,1)S(1)}, u32[]{:S(2)}, u32[]{:S(2)}) collective-permute-start(bf16[64,3712]{1,0:T(8,128)(2,1)S(1)} %get-tuple-element.140), channel_id=1, source_target_pairs={{0,496},{16,0},{32,16},{48,32},{64,48},{80,64},{96,80},{112,96},{1... | collective-permute-start | bytes 1425416 | tf_op jit(solution)/shard_map/ppermute | solution.py:197
  104.8 21.0 %collective-permute-start.22 = (bf16[64,3712]{1,0:T(8,128)(2,1)}, bf16[64,3712]{1,0:T(8,128)(2,1)S(1)}, u32[]{:S(2)}, u32[]{:S(2)}) collective-permute-start(bf16[64,3712]{1,0:T(8,128)(2,1)} %collective-permute-done.17.refs_2_), channel_id=1, source_target_pairs={{0,1},{1,2},{2,3},{3,4},{4,5},{5,6},{6,7},{7,8},{8,9},{9,10},{10,1... | collective-permute-start | bytes 1425416 | tf_op jit(solution)/shard_map/ppermute | solution.py:174
  109.4 20.8 %collective-permute-start.19 = (bf16[64,3712]{1,0:T(8,128)(2,1)}, bf16[64,3712]{1,0:T(8,128)(2,1)S(1)}, u32[]{:S(2)}, u32[]{:S(2)}) collective-permute-start(bf16[64,3712]{1,0:T(8,128)(2,1)} %collective-permute-done.15.refs_0_), channel_id=1, source_target_pairs={{0,15},{1,0},{2,1},{3,2},{4,3},{5,4},{6,5},{7,6},{8,7},{9,8},{10,9... | collective-permute-start | bytes 1425416 | tf_op jit(solution)/shard_map/ppermute | solution.py:172
  114.1 20.7 %collective-permute-start.28 = (bf16[64,3584]{1,0:T(8,128)(2,1)}, bf16[64,3584]{1,0:T(8,128)(2,1)S(1)}, u32[]{:S(2)}, u32[]{:S(2)}) collective-permute-start(bf16[64,3584]{1,0:T(8,128)(2,1)} %collective-permute-done.23.refs_3_), channel_id=1, source_target_pairs={{0,1},{1,2},{2,3},{3,4},{4,5},{5,6},{6,7},{7,8},{8,9},{9,10},{10,1... | collective-permute-start | bytes 1376264 | tf_op jit(solution)/shard_map/ppermute | solution.py:174
  116.0 20.9 %collective-permute-start.26 = (bf16[64,3584]{1,0:T(8,128)(2,1)S(1)}, bf16[64,3584]{1,0:T(8,128)(2,1)S(1)}, u32[]{:S(2)}, u32[]{:S(2)}) collective-permute-start(bf16[64,3584]{1,0:T(8,128)(2,1)S(1)} %get-tuple-element.151), channel_id=1, source_target_pairs={{0,496},{16,0},{32,16},{48,32},{64,48},{80,64},{96,80},{112,96},{1... | collective-permute-start | bytes 1376264 | tf_op jit(solution)/shard_map/ppermute | solution.py:197
  145.3 23.0 %collective-permute-start.32 = (bf16[64,3712]{1,0:T(8,128)(2,1)S(1)}, bf16[64,3712]{1,0:T(8,128)(2,1)S(1)}, u32[]{:S(2)}, u32[]{:S(2)}) collective-permute-start(bf16[64,3712]{1,0:T(8,128)(2,1)S(1)} %collective-permute-done.24.refs_0_), channel_id=1, source_target_pairs={{0,15},{1,0},{2,1},{3,2},{4,3},{5,4},{6,5},{7,6},{8,7},{9,8},{10,9... | collective-permute-start | bytes 1425416 | tf_op jit(solution)/shard_map/ppermute | solution.py:172
  155.7 22.8 %collective-permute-start.30 = (bf16[64,3712]{1,0:T(8,128)(2,1)S(1)}, bf16[64,3712]{1,0:T(8,128)(2,1)S(1)}, u32[]{:S(2)}, u32[]{:S(2)}) collective-permute-start(bf16[64,3712]{1,0:T(8,128)(2,1)S(1)} %collective-permute-done.27.refs_2_), channel_id=1, source_target_pairs={{0,1},{1,2},{2,3},{3,4},{4,5},{5,6},{6,7},{7,8},{8,9},{9,10},{10,1... | collective-permute-start | bytes 1425416 | tf_op jit(solution)/shard_map/ppermute | solution.py:174
  198.9 19.8 %collective-permute-start.50 = (bf16[64,3584]{1,0:T(8,128)(2,1)S(1)}, bf16[64,3584]{1,0:T(8,128)(2,1)S(1)}, u32[]{:S(2)}, u32[]{:S(2)}) collective-permute-start(bf16[64,3584]{1,0:T(8,128)(2,1)S(1)} %shard_map.143), channel_id=1, source_target_pairs={{0,1},{1,2},{2,3},{3,4},{4,5},{5,6},{6,7},{7,8},{8,9},{9,10},{10,1... | collective-permute-start | bytes 1376264 | tf_op jit(solution)/shard_map/ppermute | solution.py:236
  207.6 19.4 %collective-permute-start.36 = (bf16[64,3584]{1,0:T(8,128)(2,1)S(1)}, bf16[64,3584]{1,0:T(8,128)(2,1)S(1)}, u32[]{:S(2)}, u32[]{:S(2)}) collective-permute-start(bf16[64,3584]{1,0:T(8,128)(2,1)S(1)} %shard_map.128), channel_id=1, source_target_pairs={{0,1},{1,2},{2,3},{3,4},{4,5},{5,6},{6,7},{7,8},{8,9},{9,10},{10,1... | collective-permute-start | bytes 1376264 | tf_op jit(solution)/shard_map/ppermute | solution.py:236
  227.2 19.4 %collective-permute-start.37 = (bf16[64,3584]{1,0:T(8,128)(2,1)S(1)}, bf16[64,3584]{1,0:T(8,128)(2,1)S(1)}, u32[]{:S(2)}, u32[]{:S(2)}) collective-permute-start(bf16[64,3584]{1,0:T(8,128)(2,1)S(1)} %shard_map.129), channel_id=1, source_target_pairs={{0,1},{1,2},{2,3},{3,4},{4,5},{5,6},{6,7},{7,8},{8,9},{9,10},{10,1... | collective-permute-start | bytes 1376264 | tf_op jit(solution)/shard_map/ppermute | solution.py:236
  246.9 19.4 %collective-permute-start.38 = (bf16[64,3584]{1,0:T(8,128)(2,1)S(1)}, bf16[64,3584]{1,0:T(8,128)(2,1)S(1)}, u32[]{:S(2)}, u32[]{:S(2)}) collective-permute-start(bf16[64,3584]{1,0:T(8,128)(2,1)S(1)} %shard_map.130), channel_id=1, source_target_pairs={{0,1},{1,2},{2,3},{3,4},{4,5},{5,6},{6,7},{7,8},{8,9},{9,10},{10,1... | collective-permute-start | bytes 1376264 | tf_op jit(solution)/shard_map/ppermute | solution.py:236
  257.6 19.4 %collective-permute-start.53 = (bf16[64,3584]{1,0:T(8,128)(2,1)S(1)}, bf16[64,3584]{1,0:T(8,128)(2,1)S(1)}, u32[]{:S(2)}, u32[]{:S(2)}) collective-permute-start(bf16[64,3584]{1,0:T(8,128)(2,1)S(1)} %shard_map.146), channel_id=1, source_target_pairs={{0,1},{1,2},{2,3},{3,4},{4,5},{5,6},{6,7},{7,8},{8,9},{9,10},{10,1... | collective-permute-start | bytes 1376264 | tf_op jit(solution)/shard_map/ppermute | solution.py:236
  266.6 19.4 %collective-permute-start.39 = (bf16[64,3584]{1,0:T(8,128)(2,1)S(1)}, bf16[64,3584]{1,0:T(8,128)(2,1)S(1)}, u32[]{:S(2)}, u32[]{:S(2)}) collective-permute-start(bf16[64,3584]{1,0:T(8,128)(2,1)S(1)} %shard_map.131), channel_id=1, source_target_pairs={{0,1},{1,2},{2,3},{3,4},{4,5},{5,6},{6,7},{7,8},{8,9},{9,10},{10,1... | collective-permute-start | bytes 1376264 | tf_op jit(solution)/shard_map/ppermute | solution.py:236
  268.8 19.6 %collective-permute-start.61 = (bf16[64,3584]{1,0:T(8,128)(2,1)S(1)}, bf16[64,3584]{1,0:T(8,128)(2,1)S(1)}, u32[]{:S(2)}, u32[]{:S(2)}) collective-permute-start(bf16[64,3584]{1,0:T(8,128)(2,1)S(1)} %shard_map.154), channel_id=1, source_target_pairs={{0,15},{1,0},{2,1},{3,2},{4,3},{5,4},{6,5},{7,6},{8,7},{9,8},{10,9... | collective-permute-start | bytes 1376264 | tf_op jit(solution)/shard_map/ppermute | solution.py:242
  273.7 19.6 %collective-permute-start.47 = (bf16[64,3584]{1,0:T(8,128)(2,1)S(1)}, bf16[64,3584]{1,0:T(8,128)(2,1)S(1)}, u32[]{:S(2)}, u32[]{:S(2)}) collective-permute-start(bf16[64,3584]{1,0:T(8,128)(2,1)S(1)} %shard_map.139), channel_id=1, source_target_pairs={{0,15},{1,0},{2,1},{3,2},{4,3},{5,4},{6,5},{7,6},{8,7},{9,8},{10,9... | collective-permute-start | bytes 1376264 | tf_op jit(solution)/shard_map/ppermute | solution.py:242
  277.2 26.2 %collective-permute-start.54 = (bf16[64,3584]{1,0:T(8,128)(2,1)S(1)}, bf16[64,3584]{1,0:T(8,128)(2,1)S(1)}, u32[]{:S(2)}, u32[]{:S(2)}) collective-permute-start(bf16[64,3584]{1,0:T(8,128)(2,1)S(1)} %shard_map.147), channel_id=1, source_target_pairs={{0,1},{1,2},{2,3},{3,4},{4,5},{5,6},{6,7},{7,8},{8,9},{9,10},{10,1... | collective-permute-start | bytes 1376264 | tf_op jit(solution)/shard_map/ppermute | solution.py:236
  286.2 19.4 %collective-permute-start.40 = (bf16[64,3584]{1,0:T(8,128)(2,1)S(1)}, bf16[64,3584]{1,0:T(8,128)(2,1)S(1)}, u32[]{:S(2)}, u32[]{:S(2)}) collective-permute-start(bf16[64,3584]{1,0:T(8,128)(2,1)S(1)} %shard_map.132), channel_id=1, source_target_pairs={{0,1},{1,2},{2,3},{3,4},{4,5},{5,6},{6,7},{7,8},{8,9},{9,10},{10,1... | collective-permute-start | bytes 1376264 | tf_op jit(solution)/shard_map/ppermute | solution.py:236
  288.7 21.7 %collective-permute-start.62 = (bf16[64,3584]{1,0:T(8,128)(2,1)S(1)}, bf16[64,3584]{1,0:T(8,128)(2,1)S(1)}, u32[]{:S(2)}, u32[]{:S(2)}) collective-permute-start(bf16[64,3584]{1,0:T(8,128)(2,1)S(1)} %shard_map.155), channel_id=1, source_target_pairs={{0,15},{1,0},{2,1},{3,2},{4,3},{5,4},{6,5},{7,6},{8,7},{9,8},{10,9... | collective-permute-start | bytes 1376264 | tf_op jit(solution)/shard_map/ppermute | solution.py:242
  293.5 21.7 %collective-permute-start.48 = (bf16[64,3584]{1,0:T(8,128)(2,1)S(1)}, bf16[64,3584]{1,0:T(8,128)(2,1)S(1)}, u32[]{:S(2)}, u32[]{:S(2)}) collective-permute-start(bf16[64,3584]{1,0:T(8,128)(2,1)S(1)} %shard_map.140), channel_id=1, source_target_pairs={{0,31},{1,16},{2,17},{3,18},{4,19},{5,20},{6,21},{7,22},{8,23},{9,... | collective-permute-start | bytes 1376264 | tf_op jit(solution)/shard_map/ppermute | solution.py:228
  303.7 24.6 %collective-permute-start.55 = (bf16[64,3584]{1,0:T(8,128)(2,1)S(1)}, bf16[64,3584]{1,0:T(8,128)(2,1)S(1)}, u32[]{:S(2)}, u32[]{:S(2)}) collective-permute-start(bf16[64,3584]{1,0:T(8,128)(2,1)S(1)} %shard_map.148), channel_id=1, source_target_pairs={{0,497},{1,498},{2,499},{3,500},{4,501},{5,502},{6,503},{7,504},{8... | collective-permute-start | bytes 1376264 | tf_op jit(solution)/shard_map/ppermute | solution.py:228
  306.0 21.1 %collective-permute-start.41 = (bf16[64,3584]{1,0:T(8,128)(2,1)S(1)}, bf16[64,3584]{1,0:T(8,128)(2,1)S(1)}, u32[]{:S(2)}, u32[]{:S(2)}) collective-permute-start(bf16[64,3584]{1,0:T(8,128)(2,1)S(1)} %shard_map.133), channel_id=1, source_target_pairs={{0,17},{1,18},{2,19},{3,20},{4,21},{5,22},{6,23},{7,24},{8,25},{9,... | collective-permute-start | bytes 1376264 | tf_op jit(solution)/shard_map/ppermute | solution.py:228
  (48 other events, 744.5 us)

commit v3 on v2

--- a/solution.py
+++ b/solution.py
@@ -8,7 +8,7 @@
 EXP_SECTION = 2
 TAIL = 128
 OWN_STEP = 1
-BASE_STEPS = ((3, 4), (5, 6))
+BASE_STEPS = ((4, 5), (6, 7))
 VMEM_LIMIT = 16 * 1024 * 1024
 
 
@@ -22,20 +22,25 @@
     )
 
 
-def norm_rows(inputs, gain, tail=None):
+def norm_of(inputs, gain):
+    values = inputs.astype(jnp.float32)
+    meansq = jnp.mean(values * values, axis=-1, keepdims=True) + 1e-06
+    return (values * lax.rsqrt(meansq) * gain).astype(jnp.bfloat16)
+
+
+def norm_rows(inputs, gain, picks, other_picks):
     rows, width = inputs.shape
-    extra = 0 if tail is None else tail.shape[1]
-
-    def kernel(inputs_ref, gain_ref, *refs):
-        values = inputs_ref[...].astype(jnp.float32)
-        meansq = jnp.mean(values * values, axis=-1, keepdims=True) + 1e-06
-        refs[-1][:, :width] = (values * lax.rsqrt(meansq) * gain_ref[...]).astype(jnp.bfloat16)
-        if extra:
-            refs[-1][:, width:] = refs[0][...]
-
-    shape = jax.ShapeDtypeStruct((rows, width + extra), jnp.bfloat16)
-    operands = (inputs, gain) + (() if tail is None else (tail,))
-    return call(kernel, shape, 4 * rows * width, 4 * rows * width)(*operands)
+
+    def kernel(inputs_ref, gain_ref, picks_ref, other_ref, out_ref):
+        out_ref[:, :width] = norm_of(inputs_ref[...], gain_ref[...])
+        lane = lax.broadcasted_iota(jnp.int32, (rows, TAIL), 1)
+        routes = jnp.where(lane < TAIL // 2, picks_ref[...], other_ref[...])
+        out_ref[:, width:] = routes.astype(jnp.float32).astype(jnp.bfloat16)
+
+    shape = jax.ShapeDtypeStruct((rows, width + TAIL), jnp.bfloat16)
+    return call(kernel, shape, 50000 * rows * width, 4 * rows * width)(
+        inputs, gain, picks, other_picks
+    )
 
 
 def hidden_of(tokens, gate, up):
@@ -44,7 +49,7 @@
     return gated / (1.0 + jnp.exp(-gated)) * upper
 
 
-def hidden_rows(blocks, carriers, lanes, expert, gate, up):
+def hidden_rows(blocks, carriers, lanes, expert, gain, gate, up):
     count = len(blocks)
     width, units = gate.shape
     rows = blocks[0].shape[0]
@@ -55,10 +60,13 @@
     place = [[block is other for other in given].index(True) for block in blocks]
     bearer = [[block is other for other in given].index(True) for block in carriers]
 
-    def kernel(expert_ref, gate_ref, up_ref, *refs):
+    def kernel(expert_ref, gain_ref, gate_ref, up_ref, *refs):
         mine = expert_ref[0].astype(jnp.float32)
         for i in range(count):
-            hidden = hidden_of(refs[place[i]][:, :width], gate_ref[...], up_ref[...])
+            tokens = refs[place[i]][:, :width]
+            if blocks[i].shape[1] == width:
+                tokens = norm_of(tokens, gain_ref[...])
+            hidden = hidden_of(tokens, gate_ref[...], up_ref[...])
             picks = refs[bearer[i]][:, lanes[i] : lanes[i] + 1].astype(jnp.float32)
             refs[len(given) + i][...] = jnp.where(picks == mine, hidden, 0.0).astype(
                 jnp.bfloat16
@@ -72,8 +80,8 @@
         shape,
         flops,
         4 * width * units + 2 * count * rows * width,
-        in_specs=[pl.BlockSpec(memory_space=pltpu.SMEM)] + [vmem] * (2 + len(given)),
-    )(expert, gate, up, *given)
+        in_specs=[pl.BlockSpec(memory_space=pltpu.SMEM)] + [vmem] * (3 + len(given)),
+    )(expert, gain, gate, up, *given)
 
 
 def add_partial(hidden, down, arrived):
@@ -119,20 +127,20 @@
     )
 
 
-def finish(base, arrived):
-    high, low = base
-    rows, width = low.shape
-
-    def kernel(high_ref, low_ref, a_ref, b_ref, out_ref):
-        weight = jnp.sum(
-            high_ref[:, width:].astype(jnp.float32), axis=1, keepdims=True
-        )
-        total = a_ref[...].astype(jnp.float32) + b_ref[...].astype(jnp.float32)
-        moved = high_ref[:, :width].astype(jnp.float32) + low_ref[...].astype(jnp.float32)
-        out_ref[0] = (moved + weight * total).astype(jnp.bfloat16)
-
-    shape = jax.ShapeDtypeStruct((1, rows, width), jnp.bfloat16)
-    return call(kernel, shape, 4 * rows * width, 10 * rows * width)(high, low, *arrived)
+def finish(bases, sums):
+    rows, width = bases[0][1].shape
+
+    def kernel(*refs):
+        for way in range(2):
+            high_ref, low_ref, a_ref, b_ref = refs[4 * way : 4 * way + 4]
+            weight = jnp.sum(high_ref[:, width:].astype(jnp.float32), axis=1, keepdims=True)
+            total = a_ref[...].astype(jnp.float32) + b_ref[...].astype(jnp.float32)
+            moved = high_ref[:, :width].astype(jnp.float32) + low_ref[...].astype(jnp.float32)
+            refs[8 + way][0] = (moved + weight * total).astype(jnp.bfloat16)
+
+    shape = [jax.ShapeDtypeStruct((1, rows, width), jnp.bfloat16)] * 2
+    operands = [value for way in range(2) for value in (*bases[way], *sums[way])]
+    return call(kernel, shape, 8 * rows * width, 20 * rows * width)(*operands)
 
 
 def per_device(
@@ -154,24 +162,22 @@
     half = ring // 2
     me = lax.axis_index("expert")
     my_expert = me // (ring // EXP_SECTION)
-    forward = [(i, (i + 1) % ring) for i in range(ring)]
-    backward = [(i, (i - 1) % ring) for i in range(ring)]
+    plus = [(i, (i + 1) % ring) for i in range(ring)]
+    minus = [(i, (i - 1) % ring) for i in range(ring)]
 
     expert = my_expert.astype(jnp.int32).reshape(1)
 
-    picks = jnp.concatenate([routes_down[0], routes_up[0]], axis=1).astype(jnp.bfloat16)
-    tail = jnp.repeat(picks, TAIL // 2, axis=1)
     lanes = (width, width + TAIL // 2)
-    normed = (norm_rows(acts_down, norm_gain, tail), norm_rows(acts_up, norm_gain))
+    sent = (norm_rows(acts_down, norm_gain, routes_down[0], routes_up[0]), acts_up)
 
     hidden = [{}, {}]
-    ahead, behind = list(normed), list(normed)
+    ahead, behind = list(sent), list(sent)
     for step in range(1, half + 1):
-        for way in range(2):
+        for way in (1, 0):
             if step < half or way == 0:
-                ahead[way] = lax.ppermute(ahead[way], "expert", backward)
+                ahead[way] = lax.ppermute(ahead[way], "expert", plus)
             if step < half or way == 1:
-                behind[way] = lax.ppermute(behind[way], "expert", forward)
+                behind[way] = lax.ppermute(behind[way], "expert", minus)
             if 1 < step < half:
                 ahead[way], hidden[way][step - 1] = lax.optimization_barrier(
                     (ahead[way], hidden[way][step - 1])
@@ -185,9 +191,9 @@
                     (ahead[way], base[way][part])
                 )
         if step == OWN_STEP:
-            behind[0], *mine = lax.optimization_barrier((behind[0], *normed))
+            behind[0], *mine = lax.optimization_barrier((behind[0], *sent))
             hidden[0][0], hidden[1][0] = hidden_rows(
-                mine, (mine[0], mine[0]), lanes, expert, gate, up
+                mine, (mine[0], mine[0]), lanes, expert, norm_gain, gate, up
             )
             sections = lax.axis_size("section")
             base = [None, None]
@@ -208,12 +214,13 @@
                 (ahead[0], ahead[0], behind[0], behind[0]),
                 lanes * 2,
                 expert,
+                norm_gain,
                 gate,
                 up,
             )
         else:
             hidden[0][half], hidden[1][-half] = hidden_rows(
-                (ahead[0], behind[1]), (ahead[0], ahead[0]), lanes, expert, gate, up
+                (ahead[0], behind[1]), (ahead[0], ahead[0]), lanes, expert, norm_gain, gate, up
             )
 
     def add(way, offset, arrived):
@@ -233,16 +240,16 @@
             if step < half or way == 0:
                 onward[way] = add(way, step, onward[way])
                 if step > 1:
-                    onward[way] = lax.ppermute(onward[way], "expert", forward)
+                    onward[way] = lax.ppermute(onward[way], "expert", minus)
                 else:
-                    onward[way] = last_hop(onward[way], way, 1)
+                    onward[way] = last_hop(onward[way], way, -1)
             if step < half or way == 1:
                 returning[way] = add(way, -step, returning[way])
                 if step > 1:
-                    returning[way] = lax.ppermute(returning[way], "expert", backward)
+                    returning[way] = lax.ppermute(returning[way], "expert", plus)
                 else:
-                    returning[way] = last_hop(returning[way], way, -1)
-    return tuple(finish(base[way], (onward[way], returning[way])) for way in range(2))
+                    returning[way] = last_hop(returning[way], way, 1)
+    return tuple(finish(base, list(zip(onward, returning))))
 
 
 def solution(mesh):

time: 332 us -> 331 us (level)
  waiting for transfers between devices: 70.9 us -> 56.2 us
  starting transfers between devices: 222 us -> 235 us
    ppermute x56, waiting for transfers between devices: 59.1 us -> 43.4 us  [the longest x13 16.9 us: per_device(): onward[way] = lax.ppermute(onward[way], 'expert', minus)]
    ppermute x56, starting transfers between devices: 184 us -> 196 us  [the longest x15 72.8 us: per_device(): behind[way] = lax.ppermute(behind[way], 'expert', minus)]
  transfers between devices with their start and end apart: 64 -> 64, of which waited for: 17 -> 26; matrix products, arithmetic and copies ran while one was open for 0% -> 0% of each run, Pallas kernels for 8% -> 9%
where the time goes in v3:
time: 331 us; the launch traced here: 328 us
  starting transfers between devices  235 us (71%)
  waiting for transfers between devices  56.2 us (17%)
  Pallas kernels  30.6 us (9%)
  local copies, waits for them, and re-layouts  4.13 us (1%)
    ppermute x15, starting transfers between devices, per_device(): behind[way] = lax.ppermute(behind[way], 'expert', minus)  72.8 us
    ppermute x13, starting transfers between devices, per_device(): onward[way] = lax.ppermute(onward[way], 'expert', minus)  65.4 us
    ppermute x15, starting transfers between devices, per_device(): ahead[way] = lax.ppermute(ahead[way], 'expert', plus)  32.8 us
    ppermute x13, starting transfers between devices, per_device(): returning[way] = lax.ppermute(returning[way], 'expert', plus)  25 us
    ppermute x4, starting transfers between devices, last_hop(): return lax.ppermute(value, ('section', 'expert'), route)  21.4 us
    pallas_call x9, Pallas kernels, hidden_rows(): call(kernel, shape, flops, 4 * width * units + 2 * count * rows * width,...  19.7 us
    ppermute x4, starting transfers between devices, per_device(): lax.ppermute(part, 'section', route)  17.4 us
    ppermute x13, waiting for transfers between devices, per_device(): onward[way] = lax.ppermute(onward[way], 'expert', minus)  16.9 us
  transfers between devices with their start and end apart: 64, of which 26 were waited for; matrix products, arithmetic and copies ran while one was open for 0% of the time, Pallas kernels for 9%

profile of v3, /device:TPU:1, one launch (start us, length us, event | category | flops | bytes accessed | tf_op | source)
XLA Modules:
  0.0 327.5 jit_solution(13761314971045970462)
XLA Ops:
  4.0 4.5 %collective-permute-start = (bf16[64,3712]{1,0:T(8,128)(2,1)S(1)}, bf16[64,3712]{1,0:T(8,128)(2,1)}, u32[]{:S(2)}, u32[]{:S(2)}) collective-permute-start(bf16[64,3712]{1,0:T(8,128)(2,1)S(1)} %shard_map.113.refs_0_), channel_id=1, source_target_pairs={{0,1},{1,2},{2,3},{3,4},{4,5},{5,6},{6,7},{7,8},{8,9},{9,10},{10,1... | collective-permute-start | bytes 1425416 | tf_op jit(solution)/shard_map/ppermute | solution.py:178
  8.5 9.5 %collective-permute-start.4 = (bf16[64,3584]{1,0:T(8,128)(2,1)S(1)}, bf16[64,3584]{1,0:T(8,128)(2,1)}, u32[]{:S(2)}, u32[]{:S(2)}) collective-permute-start(bf16[64,3584]{1,0:T(8,128)(2,1)S(1)} %bitcast.60), channel_id=1, source_target_pairs={{0,15},{1,0},{2,1},{3,2},{4,3},{5,4},{6,5},{7,6},{8,7},{9,8},{10,9... | collective-permute-start | bytes 1376264 | tf_op jit(solution)/shard_map/ppermute | solution.py:180
  28.7 4.6 %collective-permute-start.8 = (bf16[64,3584]{1,0:T(8,128)(2,1)}, bf16[64,3584]{1,0:T(8,128)(2,1)}, u32[]{:S(2)}, u32[]{:S(2)}) collective-permute-start(bf16[64,3584]{1,0:T(8,128)(2,1)} %collective-permute-done.4.refs_3_), channel_id=1, source_target_pairs={{0,15},{1,0},{2,1},{3,2},{4,3},{5,4},{6,5},{7,6},{8,7},{9,8},{10,9... | collective-permute-start | bytes 1376264 | tf_op jit(solution)/shard_map/ppermute | solution.py:180
  37.6 5.2 %collective-permute-start.7 = (bf16[64,3712]{1,0:T(8,128)(2,1)}, bf16[64,3712]{1,0:T(8,128)(2,1)}, u32[]{:S(2)}, u32[]{:S(2)}) collective-permute-start(bf16[64,3712]{1,0:T(8,128)(2,1)} %collective-permute-done.3.refs_2_), channel_id=1, source_target_pairs={{0,15},{1,0},{2,1},{3,2},{4,3},{5,4},{6,5},{7,6},{8,7},{9,8},{10,9... | collective-permute-start | bytes 1425416 | tf_op jit(solution)/shard_map/ppermute | solution.py:180
  47.8 4.9 %collective-permute-start.12 = (bf16[64,3584]{1,0:T(8,128)(2,1)}, bf16[64,3584]{1,0:T(8,128)(2,1)}, u32[]{:S(2)}, u32[]{:S(2)}) collective-permute-start(bf16[64,3584]{1,0:T(8,128)(2,1)} %collective-permute-done.8.refs_3_), channel_id=1, source_target_pairs={{0,15},{1,0},{2,1},{3,2},{4,3},{5,4},{6,5},{7,6},{8,7},{9,8},{10,9... | collective-permute-start | bytes 1376264 | tf_op jit(solution)/shard_map/ppermute | solution.py:180
  57.7 5.3 %collective-permute-start.11 = (bf16[64,3712]{1,0:T(8,128)(2,1)}, bf16[64,3712]{1,0:T(8,128)(2,1)S(1)}, u32[]{:S(2)}, u32[]{:S(2)}) collective-permute-start(bf16[64,3712]{1,0:T(8,128)(2,1)} %collective-permute-done.7.refs_2_), channel_id=1, source_target_pairs={{0,15},{1,0},{2,1},{3,2},{4,3},{5,4},{6,5},{7,6},{8,7},{9,8},{10,9... | collective-permute-start | bytes 1425416 | tf_op jit(solution)/shard_map/ppermute | solution.py:180
  68.2 6.9 %collective-permute-start.13 = (bf16[64,3712]{1,0:T(8,128)(2,1)S(1)}, bf16[64,3712]{1,0:T(8,128)(2,1)S(1)}, u32[]{:S(2)}, u32[]{:S(2)}) collective-permute-start(bf16[64,3712]{1,0:T(8,128)(2,1)S(1)} %get-tuple-element.119), channel_id=1, source_target_pairs={{0,16},{16,32},{32,48},{48,64},{64,80},{80,96},{96,112},{112,128},... | collective-permute-start | bytes 1425416 | tf_op jit(solution)/shard_map/ppermute | solution.py:203
  75.1 4.9 %collective-permute-start.17 = (bf16[64,3584]{1,0:T(8,128)(2,1)}, bf16[64,3584]{1,0:T(8,128)(2,1)S(1)}, u32[]{:S(2)}, u32[]{:S(2)}) collective-permute-start(bf16[64,3584]{1,0:T(8,128)(2,1)} %collective-permute-done.12.refs_3_), channel_id=1, source_target_pairs={{0,15},{1,0},{2,1},{3,2},{4,3},{5,4},{6,5},{7,6},{8,7},{9,8},{10,9... | collective-permute-start | bytes 1376264 | tf_op jit(solution)/shard_map/ppermute | solution.py:180
  81.9 4.6 %collective-permute-start.16 = (bf16[64,3712]{1,0:T(8,128)(2,1)S(1)}, bf16[64,3712]{1,0:T(8,128)(2,1)}, u32[]{:S(2)}, u32[]{:S(2)}) collective-permute-start(bf16[64,3712]{1,0:T(8,128)(2,1)S(1)} %collective-permute-done.11.refs_2_), channel_id=1, source_target_pairs={{0,15},{1,0},{2,1},{3,2},{4,3},{5,4},{6,5},{7,6},{8,7},{9,8},{10,9... | collective-permute-start | bytes 1425416 | tf_op jit(solution)/shard_map/ppermute | solution.py:180
  94.6 4.9 %collective-permute-start.22 = (bf16[64,3584]{1,0:T(8,128)(2,1)S(1)}, bf16[64,3584]{1,0:T(8,128)(2,1)}, u32[]{:S(2)}, u32[]{:S(2)}) collective-permute-start(bf16[64,3584]{1,0:T(8,128)(2,1)S(1)} %collective-permute-done.17.refs_3_), channel_id=1, source_target_pairs={{0,15},{1,0},{2,1},{3,2},{4,3},{5,4},{6,5},{7,6},{8,7},{9,8},{10,9... | collective-permute-start | bytes 1376264 | tf_op jit(solution)/shard_map/ppermute | solution.py:180
  101.4 4.7 %collective-permute-start.21 = (bf16[64,3712]{1,0:T(8,128)(2,1)}, bf16[64,3712]{1,0:T(8,128)(2,1)}, u32[]{:S(2)}, u32[]{:S(2)}) collective-permute-start(bf16[64,3712]{1,0:T(8,128)(2,1)} %collective-permute-done.16.refs_2_), channel_id=1, source_target_pairs={{0,15},{1,0},{2,1},{3,2},{4,3},{5,4},{6,5},{7,6},{8,7},{9,8},{10,9... | collective-permute-start | bytes 1425416 | tf_op jit(solution)/shard_map/ppermute | solution.py:180
  111.4 4.6 %collective-permute-start.27 = (bf16[64,3584]{1,0:T(8,128)(2,1)}, bf16[64,3584]{1,0:T(8,128)(2,1)}, u32[]{:S(2)}, u32[]{:S(2)}) collective-permute-start(bf16[64,3584]{1,0:T(8,128)(2,1)} %collective-permute-done.22.refs_3_), channel_id=1, source_target_pairs={{0,15},{1,0},{2,1},{3,2},{4,3},{5,4},{6,5},{7,6},{8,7},{9,8},{10,9... | collective-permute-start | bytes 1376264 | tf_op jit(solution)/shard_map/ppermute | solution.py:180
  121.9 4.6 %collective-permute-start.26 = (bf16[64,3712]{1,0:T(8,128)(2,1)}, bf16[64,3712]{1,0:T(8,128)(2,1)S(1)}, u32[]{:S(2)}, u32[]{:S(2)}) collective-permute-start(bf16[64,3712]{1,0:T(8,128)(2,1)} %collective-permute-done.21.refs_2_), channel_id=1, source_target_pairs={{0,15},{1,0},{2,1},{3,2},{4,3},{5,4},{6,5},{7,6},{8,7},{9,8},{10,9... | collective-permute-start | bytes 1425416 | tf_op jit(solution)/shard_map/ppermute | solution.py:180
  131.3 4.8 %collective-permute-start.31 = (bf16[64,3584]{1,0:T(8,128)(2,1)}, bf16[64,3584]{1,0:T(8,128)(2,1)S(1)}, u32[]{:S(2)}, u32[]{:S(2)}) collective-permute-start(bf16[64,3584]{1,0:T(8,128)(2,1)} %collective-permute-done.27.refs_3_), channel_id=1, source_target_pairs={{0,15},{1,0},{2,1},{3,2},{4,3},{5,4},{6,5},{7,6},{8,7},{9,8},{10,9... | collective-permute-start | bytes 1376264 | tf_op jit(solution)/shard_map/ppermute | solution.py:180
  136.1 3.7 %collective-permute-done.26.refs_2_ = bf16[64,3712]{1,0:T(8,128)(2,1)S(1)} collective-permute-done((bf16[64,3712]{1,0:T(8,128)(2,1)}, bf16[64,3712]{1,0:T(8,128)(2,1)S(1)}, u32[]{:S(2)}, u32[]{:S(2)}) %collective-permute-start.26) | collective-permute-done | bytes 475168 | tf_op jit(solution)/shard_map/ppermute | solution.py:180
  149.6 5.2 %collective-permute-start.33 = (bf16[64,3584]{1,0:T(8,128)(2,1)S(1)}, bf16[64,3584]{1,0:T(8,128)(2,1)S(1)}, u32[]{:S(2)}, u32[]{:S(2)}) collective-permute-start(bf16[64,3584]{1,0:T(8,128)(2,1)S(1)} %collective-permute-done.31.refs_3_), channel_id=1, source_target_pairs={{0,15},{1,0},{2,1},{3,2},{4,3},{5,4},{6,5},{7,6},{8,7},{9,8},{10,9... | collective-permute-start | bytes 1376264 | tf_op jit(solution)/shard_map/ppermute | solution.py:180
  165.1 5.3 %collective-permute-start.34 = (bf16[64,3584]{1,0:T(8,128)(2,1)S(1)}, bf16[64,3584]{1,0:T(8,128)(2,1)S(1)}, u32[]{:S(2)}, u32[]{:S(2)}) collective-permute-start(bf16[64,3584]{1,0:T(8,128)(2,1)S(1)} %shard_map.125), channel_id=1, source_target_pairs={{0,15},{1,0},{2,1},{3,2},{4,3},{5,4},{6,5},{7,6},{8,7},{9,8},{10,9... | collective-permute-start | bytes 1376264 | tf_op jit(solution)/shard_map/ppermute | solution.py:243
  178.1 5.3 %collective-permute-start.49 = (bf16[64,3584]{1,0:T(8,128)(2,1)S(1)}, bf16[64,3584]{1,0:T(8,128)(2,1)S(1)}, u32[]{:S(2)}, u32[]{:S(2)}) collective-permute-start(bf16[64,3584]{1,0:T(8,128)(2,1)S(1)} %shard_map.140), channel_id=1, source_target_pairs={{0,15},{1,0},{2,1},{3,2},{4,3},{5,4},{6,5},{7,6},{8,7},{9,8},{10,9... | collective-permute-start | bytes 1376264 | tf_op jit(solution)/shard_map/ppermute | solution.py:243
  184.2 5.3 %collective-permute-start.35 = (bf16[64,3584]{1,0:T(8,128)(2,1)S(1)}, bf16[64,3584]{1,0:T(8,128)(2,1)S(1)}, u32[]{:S(2)}, u32[]{:S(2)}) collective-permute-start(bf16[64,3584]{1,0:T(8,128)(2,1)S(1)} %shard_map.126), channel_id=1, source_target_pairs={{0,15},{1,0},{2,1},{3,2},{4,3},{5,4},{6,5},{7,6},{8,7},{9,8},{10,9... | collective-permute-start | bytes 1376264 | tf_op jit(solution)/shard_map/ppermute | solution.py:243
  194.9 4.6 %collective-permute-start.50 = (bf16[64,3584]{1,0:T(8,128)(2,1)S(1)}, bf16[64,3584]{1,0:T(8,128)(2,1)S(1)}, u32[]{:S(2)}, u32[]{:S(2)}) collective-permute-start(bf16[64,3584]{1,0:T(8,128)(2,1)S(1)} %shard_map.141), channel_id=1, source_target_pairs={{0,15},{1,0},{2,1},{3,2},{4,3},{5,4},{6,5},{7,6},{8,7},{9,8},{10,9... | collective-permute-start | bytes 1376264 | tf_op jit(solution)/shard_map/ppermute | solution.py:243
  202.9 5.3 %collective-permute-start.36 = (bf16[64,3584]{1,0:T(8,128)(2,1)S(1)}, bf16[64,3584]{1,0:T(8,128)(2,1)S(1)}, u32[]{:S(2)}, u32[]{:S(2)}) collective-permute-start(bf16[64,3584]{1,0:T(8,128)(2,1)S(1)} %shard_map.127), channel_id=1, source_target_pairs={{0,15},{1,0},{2,1},{3,2},{4,3},{5,4},{6,5},{7,6},{8,7},{9,8},{10,9... | collective-permute-start | bytes 1376264 | tf_op jit(solution)/shard_map/ppermute | solution.py:243
  215.1 4.6 %collective-permute-start.51 = (bf16[64,3584]{1,0:T(8,128)(2,1)S(1)}, bf16[64,3584]{1,0:T(8,128)(2,1)S(1)}, u32[]{:S(2)}, u32[]{:S(2)}) collective-permute-start(bf16[64,3584]{1,0:T(8,128)(2,1)S(1)} %shard_map.142), channel_id=1, source_target_pairs={{0,15},{1,0},{2,1},{3,2},{4,3},{5,4},{6,5},{7,6},{8,7},{9,8},{10,9... | collective-permute-start | bytes 1376264 | tf_op jit(solution)/shard_map/ppermute | solution.py:243
  222.6 5.3 %collective-permute-start.37 = (bf16[64,3584]{1,0:T(8,128)(2,1)S(1)}, bf16[64,3584]{1,0:T(8,128)(2,1)S(1)}, u32[]{:S(2)}, u32[]{:S(2)}) collective-permute-start(bf16[64,3584]{1,0:T(8,128)(2,1)S(1)} %shard_map.128), channel_id=1, source_target_pairs={{0,15},{1,0},{2,1},{3,2},{4,3},{5,4},{6,5},{7,6},{8,7},{9,8},{10,9... | collective-permute-start | bytes 1376264 | tf_op jit(solution)/shard_map/ppermute | solution.py:243
  233.9 4.6 %collective-permute-start.52 = (bf16[64,3584]{1,0:T(8,128)(2,1)S(1)}, bf16[64,3584]{1,0:T(8,128)(2,1)S(1)}, u32[]{:S(2)}, u32[]{:S(2)}) collective-permute-start(bf16[64,3584]{1,0:T(8,128)(2,1)S(1)} %shard_map.143), channel_id=1, source_target_pairs={{0,15},{1,0},{2,1},{3,2},{4,3},{5,4},{6,5},{7,6},{8,7},{9,8},{10,9... | collective-permute-start | bytes 1376264 | tf_op jit(solution)/shard_map/ppermute | solution.py:243
  242.3 5.3 %collective-permute-start.38 = (bf16[64,3584]{1,0:T(8,128)(2,1)S(1)}, bf16[64,3584]{1,0:T(8,128)(2,1)S(1)}, u32[]{:S(2)}, u32[]{:S(2)}) collective-permute-start(bf16[64,3584]{1,0:T(8,128)(2,1)S(1)} %shard_map.129), channel_id=1, source_target_pairs={{0,15},{1,0},{2,1},{3,2},{4,3},{5,4},{6,5},{7,6},{8,7},{9,8},{10,9... | collective-permute-start | bytes 1376264 | tf_op jit(solution)/shard_map/ppermute | solution.py:243
  253.5 4.6 %collective-permute-start.53 = (bf16[64,3584]{1,0:T(8,128)(2,1)S(1)}, bf16[64,3584]{1,0:T(8,128)(2,1)S(1)}, u32[]{:S(2)}, u32[]{:S(2)}) collective-permute-start(bf16[64,3584]{1,0:T(8,128)(2,1)S(1)} %shard_map.144), channel_id=1, source_target_pairs={{0,15},{1,0},{2,1},{3,2},{4,3},{5,4},{6,5},{7,6},{8,7},{9,8},{10,9... | collective-permute-start | bytes 1376264 | tf_op jit(solution)/shard_map/ppermute | solution.py:243
  261.9 5.3 %collective-permute-start.39 = (bf16[64,3584]{1,0:T(8,128)(2,1)S(1)}, bf16[64,3584]{1,0:T(8,128)(2,1)S(1)}, u32[]{:S(2)}, u32[]{:S(2)}) collective-permute-start(bf16[64,3584]{1,0:T(8,128)(2,1)S(1)} %shard_map.130), channel_id=1, source_target_pairs={{0,15},{1,0},{2,1},{3,2},{4,3},{5,4},{6,5},{7,6},{8,7},{9,8},{10,9... | collective-permute-start | bytes 1376264 | tf_op jit(solution)/shard_map/ppermute | solution.py:243
  273.2 4.6 %collective-permute-start.54 = (bf16[64,3584]{1,0:T(8,128)(2,1)S(1)}, bf16[64,3584]{1,0:T(8,128)(2,1)S(1)}, u32[]{:S(2)}, u32[]{:S(2)}) collective-permute-start(bf16[64,3584]{1,0:T(8,128)(2,1)S(1)} %shard_map.145), channel_id=1, source_target_pairs={{0,15},{1,0},{2,1},{3,2},{4,3},{5,4},{6,5},{7,6},{8,7},{9,8},{10,9... | collective-permute-start | bytes 1376264 | tf_op jit(solution)/shard_map/ppermute | solution.py:243
  281.6 5.3 %collective-permute-start.40 = (bf16[64,3584]{1,0:T(8,128)(2,1)S(1)}, bf16[64,3584]{1,0:T(8,128)(2,1)S(1)}, u32[]{:S(2)}, u32[]{:S(2)}) collective-permute-start(bf16[64,3584]{1,0:T(8,128)(2,1)S(1)} %shard_map.131), channel_id=1, source_target_pairs={{0,15},{1,0},{2,1},{3,2},{4,3},{5,4},{6,5},{7,6},{8,7},{9,8},{10,9... | collective-permute-start | bytes 1376264 | tf_op jit(solution)/shard_map/ppermute | solution.py:243
  290.6 9.5 %collective-permute-start.48 = (bf16[64,3584]{1,0:T(8,128)(2,1)S(1)}, bf16[64,3584]{1,0:T(8,128)(2,1)S(1)}, u32[]{:S(2)}, u32[]{:S(2)}) collective-permute-start(bf16[64,3584]{1,0:T(8,128)(2,1)S(1)} %shard_map.139), channel_id=1, source_target_pairs={{0,17},{1,18},{2,19},{3,20},{4,21},{5,22},{6,23},{7,24},{8,25},{9,... | collective-permute-start | bytes 1376264 | tf_op jit(solution)/shard_map/ppermute | solution.py:235
  302.7 8.0 %collective-permute-start.41 = (bf16[64,3584]{1,0:T(8,128)(2,1)S(1)}, bf16[64,3584]{1,0:T(8,128)(2,1)S(1)}, u32[]{:S(2)}, u32[]{:S(2)}) collective-permute-start(bf16[64,3584]{1,0:T(8,128)(2,1)S(1)} %shard_map.132), channel_id=1, source_target_pairs={{0,31},{1,16},{2,17},{3,18},{4,19},{5,20},{6,21},{7,22},{8,23},{9,... | collective-permute-start | bytes 1376264 | tf_op jit(solution)/shard_map/ppermute | solution.py:235
  316.4 6.5 %collective-permute-done.41.refs_2_ = bf16[64,3584]{1,0:T(8,128)(2,1)S(1)} collective-permute-done((bf16[64,3584]{1,0:T(8,128)(2,1)S(1)}, bf16[64,3584]{1,0:T(8,128)(2,1)S(1)}, u32[]{:S(2)}, u32[]{:S(2)}) %collective-permute-start.41) | collective-permute-done | bytes 458784 | tf_op jit(solution)/shard_map/ppermute | solution.py:235
  (173 shorter events, 153.6 us)
Async XLA Ops:
  4.0 22.8 %collective-permute-start = (bf16[64,3712]{1,0:T(8,128)(2,1)S(1)}, bf16[64,3712]{1,0:T(8,128)(2,1)}, u32[]{:S(2)}, u32[]{:S(2)}) collective-permute-start(bf16[64,3712]{1,0:T(8,128)(2,1)S(1)} %shard_map.113.refs_0_), channel_id=1, source_target_pairs={{0,1},{1,2},{2,3},{3,4},{4,5},{5,6},{6,7},{7,8},{8,9},{9,10},{10,1... | collective-permute-start | bytes 1425416 | tf_op jit(solution)/shard_map/ppermute | solution.py:178
  8.5 20.2 %collective-permute-start.4 = (bf16[64,3584]{1,0:T(8,128)(2,1)S(1)}, bf16[64,3584]{1,0:T(8,128)(2,1)}, u32[]{:S(2)}, u32[]{:S(2)}) collective-permute-start(bf16[64,3584]{1,0:T(8,128)(2,1)S(1)} %bitcast.60), channel_id=1, source_target_pairs={{0,15},{1,0},{2,1},{3,2},{4,3},{5,4},{6,5},{7,6},{8,7},{9,8},{10,9... | collective-permute-start | bytes 1376264 | tf_op jit(solution)/shard_map/ppermute | solution.py:180
  18.0 19.6 %collective-permute-start.3 = (bf16[64,3712]{1,0:T(8,128)(2,1)S(1)}, bf16[64,3712]{1,0:T(8,128)(2,1)}, u32[]{:S(2)}, u32[]{:S(2)}) collective-permute-start(bf16[64,3712]{1,0:T(8,128)(2,1)S(1)} %shard_map.113.refs_0_), channel_id=1, source_target_pairs={{0,15},{1,0},{2,1},{3,2},{4,3},{5,4},{6,5},{7,6},{8,7},{9,8},{10,9... | collective-permute-start | bytes 1425416 | tf_op jit(solution)/shard_map/ppermute | solution.py:180
  35.7 20.0 %collective-permute-start.6 = (bf16[64,3584]{1,0:T(8,128)(2,1)}, bf16[64,3584]{1,0:T(8,128)(2,1)}, u32[]{:S(2)}, u32[]{:S(2)}) collective-permute-start(bf16[64,3584]{1,0:T(8,128)(2,1)} %collective-permute-done.2.refs_1_), channel_id=1, source_target_pairs={{0,1},{1,2},{2,3},{3,4},{4,5},{5,6},{6,7},{7,8},{8,9},{9,10},{10,1... | collective-permute-start | bytes 1376264 | tf_op jit(solution)/shard_map/ppermute | solution.py:178
  37.6 20.0 %collective-permute-start.7 = (bf16[64,3712]{1,0:T(8,128)(2,1)}, bf16[64,3712]{1,0:T(8,128)(2,1)}, u32[]{:S(2)}, u32[]{:S(2)}) collective-permute-start(bf16[64,3712]{1,0:T(8,128)(2,1)} %collective-permute-done.3.refs_2_), channel_id=1, source_target_pairs={{0,15},{1,0},{2,1},{3,2},{4,3},{5,4},{6,5},{7,6},{8,7},{9,8},{10,9... | collective-permute-start | bytes 1425416 | tf_op jit(solution)/shard_map/ppermute | solution.py:180
  45.9 20.0 %collective-permute-start.5 = (bf16[64,3712]{1,0:T(8,128)(2,1)}, bf16[64,3712]{1,0:T(8,128)(2,1)}, u32[]{:S(2)}, u32[]{:S(2)}) collective-permute-start(bf16[64,3712]{1,0:T(8,128)(2,1)} %collective-permute-done.1.refs_0_), channel_id=1, source_target_pairs={{0,1},{1,2},{2,3},{3,4},{4,5},{5,6},{6,7},{7,8},{8,9},{9,10},{10,1... | collective-permute-start | bytes 1425416 | tf_op jit(solution)/shard_map/ppermute | solution.py:178
  47.8 27.3 %collective-permute-start.12 = (bf16[64,3584]{1,0:T(8,128)(2,1)}, bf16[64,3584]{1,0:T(8,128)(2,1)}, u32[]{:S(2)}, u32[]{:S(2)}) collective-permute-start(bf16[64,3584]{1,0:T(8,128)(2,1)} %collective-permute-done.8.refs_3_), channel_id=1, source_target_pairs={{0,15},{1,0},{2,1},{3,2},{4,3},{5,4},{6,5},{7,6},{8,7},{9,8},{10,9... | collective-permute-start | bytes 1376264 | tf_op jit(solution)/shard_map/ppermute | solution.py:180
  55.7 24.3 %collective-permute-start.10 = (bf16[64,3584]{1,0:T(8,128)(2,1)}, bf16[64,3584]{1,0:T(8,128)(2,1)S(1)}, u32[]{:S(2)}, u32[]{:S(2)}) collective-permute-start(bf16[64,3584]{1,0:T(8,128)(2,1)} %collective-permute-done.6.refs_1_), channel_id=1, source_target_pairs={{0,1},{1,2},{2,3},{3,4},{4,5},{5,6},{6,7},{7,8},{8,9},{9,10},{10,1... | collective-permute-start | bytes 1376264 | tf_op jit(solution)/shard_map/ppermute | solution.py:178
  57.7 24.3 %collective-permute-start.11 = (bf16[64,3712]{1,0:T(8,128)(2,1)}, bf16[64,3712]{1,0:T(8,128)(2,1)S(1)}, u32[]{:S(2)}, u32[]{:S(2)}) collective-permute-start(bf16[64,3712]{1,0:T(8,128)(2,1)} %collective-permute-done.7.refs_2_), channel_id=1, source_target_pairs={{0,15},{1,0},{2,1},{3,2},{4,3},{5,4},{6,5},{7,6},{8,7},{9,8},{10,9... | collective-permute-start | bytes 1425416 | tf_op jit(solution)/shard_map/ppermute | solution.py:180
  65.9 23.3 %collective-permute-start.9 = (bf16[64,3712]{1,0:T(8,128)(2,1)}, bf16[64,3712]{1,0:T(8,128)(2,1)S(1)}, u32[]{:S(2)}, u32[]{:S(2)}) collective-permute-start(bf16[64,3712]{1,0:T(8,128)(2,1)} %collective-permute-done.5.refs_0_), channel_id=1, source_target_pairs={{0,1},{1,2},{2,3},{3,4},{4,5},{5,6},{6,7},{7,8},{8,9},{9,10},{10,1... | collective-permute-start | bytes 1425416 | tf_op jit(solution)/shard_map/ppermute | solution.py:178
  68.2 21.0 %collective-permute-start.13 = (bf16[64,3712]{1,0:T(8,128)(2,1)S(1)}, bf16[64,3712]{1,0:T(8,128)(2,1)S(1)}, u32[]{:S(2)}, u32[]{:S(2)}) collective-permute-start(bf16[64,3712]{1,0:T(8,128)(2,1)S(1)} %get-tuple-element.119), channel_id=1, source_target_pairs={{0,16},{16,32},{32,48},{48,64},{64,80},{80,96},{96,112},{112,128},... | collective-permute-start | bytes 1425416 | tf_op jit(solution)/shard_map/ppermute | solution.py:203
  75.1 19.5 %collective-permute-start.17 = (bf16[64,3584]{1,0:T(8,128)(2,1)}, bf16[64,3584]{1,0:T(8,128)(2,1)S(1)}, u32[]{:S(2)}, u32[]{:S(2)}) collective-permute-start(bf16[64,3584]{1,0:T(8,128)(2,1)} %collective-permute-done.12.refs_3_), channel_id=1, source_target_pairs={{0,15},{1,0},{2,1},{3,2},{4,3},{5,4},{6,5},{7,6},{8,7},{9,8},{10,9... | collective-permute-start | bytes 1376264 | tf_op jit(solution)/shard_map/ppermute | solution.py:180
  80.0 19.4 %collective-permute-start.15 = (bf16[64,3584]{1,0:T(8,128)(2,1)S(1)}, bf16[64,3584]{1,0:T(8,128)(2,1)}, u32[]{:S(2)}, u32[]{:S(2)}) collective-permute-start(bf16[64,3584]{1,0:T(8,128)(2,1)S(1)} %collective-permute-done.10.refs_1_), channel_id=1, source_target_pairs={{0,1},{1,2},{2,3},{3,4},{4,5},{5,6},{6,7},{7,8},{8,9},{9,10},{10,1... | collective-permute-start | bytes 1376264 | tf_op jit(solution)/shard_map/ppermute | solution.py:178
  81.9 19.4 %collective-permute-start.16 = (bf16[64,3712]{1,0:T(8,128)(2,1)S(1)}, bf16[64,3712]{1,0:T(8,128)(2,1)}, u32[]{:S(2)}, u32[]{:S(2)}) collective-permute-start(bf16[64,3712]{1,0:T(8,128)(2,1)S(1)} %collective-permute-done.11.refs_2_), channel_id=1, source_target_pairs={{0,15},{1,0},{2,1},{3,2},{4,3},{5,4},{6,5},{7,6},{8,7},{9,8},{10,9... | collective-permute-start | bytes 1425416 | tf_op jit(solution)/shard_map/ppermute | solution.py:180
  89.2 19.5 %collective-permute-start.14 = (bf16[64,3712]{1,0:T(8,128)(2,1)S(1)}, bf16[64,3712]{1,0:T(8,128)(2,1)}, u32[]{:S(2)}, u32[]{:S(2)}) collective-permute-start(bf16[64,3712]{1,0:T(8,128)(2,1)S(1)} %collective-permute-done.9.refs_0_), channel_id=1, source_target_pairs={{0,1},{1,2},{2,3},{3,4},{4,5},{5,6},{6,7},{7,8},{8,9},{9,10},{10,1... | collective-permute-start | bytes 1425416 | tf_op jit(solution)/shard_map/ppermute | solution.py:178
  99.4 20.5 %collective-permute-start.20 = (bf16[64,3584]{1,0:T(8,128)(2,1)}, bf16[64,3584]{1,0:T(8,128)(2,1)}, u32[]{:S(2)}, u32[]{:S(2)}) collective-permute-start(bf16[64,3584]{1,0:T(8,128)(2,1)} %collective-permute-done.15.refs_1_), channel_id=1, source_target_pairs={{0,1},{1,2},{2,3},{3,4},{4,5},{5,6},{6,7},{7,8},{8,9},{9,10},{10,1... | collective-permute-start | bytes 1376264 | tf_op jit(solution)/shard_map/ppermute | solution.py:178
  101.4 20.5 %collective-permute-start.21 = (bf16[64,3712]{1,0:T(8,128)(2,1)}, bf16[64,3712]{1,0:T(8,128)(2,1)}, u32[]{:S(2)}, u32[]{:S(2)}) collective-permute-start(bf16[64,3712]{1,0:T(8,128)(2,1)} %collective-permute-done.16.refs_2_), channel_id=1, source_target_pairs={{0,15},{1,0},{2,1},{3,2},{4,3},{5,4},{6,5},{7,6},{8,7},{9,8},{10,9... | collective-permute-start | bytes 1425416 | tf_op jit(solution)/shard_map/ppermute | solution.py:180
  109.5 19.9 %collective-permute-start.19 = (bf16[64,3712]{1,0:T(8,128)(2,1)}, bf16[64,3712]{1,0:T(8,128)(2,1)}, u32[]{:S(2)}, u32[]{:S(2)}) collective-permute-start(bf16[64,3712]{1,0:T(8,128)(2,1)} %collective-permute-done.14.refs_0_), channel_id=1, source_target_pairs={{0,1},{1,2},{2,3},{3,4},{4,5},{5,6},{6,7},{7,8},{8,9},{9,10},{10,1... | collective-permute-start | bytes 1425416 | tf_op jit(solution)/shard_map/ppermute | solution.py:178
  111.4 19.9 %collective-permute-start.27 = (bf16[64,3584]{1,0:T(8,128)(2,1)}, bf16[64,3584]{1,0:T(8,128)(2,1)}, u32[]{:S(2)}, u32[]{:S(2)}) collective-permute-start(bf16[64,3584]{1,0:T(8,128)(2,1)} %collective-permute-done.22.refs_3_), channel_id=1, source_target_pairs={{0,15},{1,0},{2,1},{3,2},{4,3},{5,4},{6,5},{7,6},{8,7},{9,8},{10,9... | collective-permute-start | bytes 1376264 | tf_op jit(solution)/shard_map/ppermute | solution.py:180
  116.5 19.6 %collective-permute-start.25 = (bf16[64,3712]{1,0:T(8,128)(2,1)S(1)}, bf16[64,3712]{1,0:T(8,128)(2,1)S(1)}, u32[]{:S(2)}, u32[]{:S(2)}) collective-permute-start(bf16[64,3712]{1,0:T(8,128)(2,1)S(1)} %get-tuple-element.149), channel_id=1, source_target_pairs={{0,496},{16,0},{32,16},{48,32},{64,48},{80,64},{96,80},{112,96},{1... | collective-permute-start | bytes 1425416 | tf_op jit(solution)/shard_map/ppermute | solution.py:203
  192.7 19.9 %collective-permute-start.43 = (bf16[64,3584]{1,0:T(8,128)(2,1)S(1)}, bf16[64,3584]{1,0:T(8,128)(2,1)S(1)}, u32[]{:S(2)}, u32[]{:S(2)}) collective-permute-start(bf16[64,3584]{1,0:T(8,128)(2,1)S(1)} %shard_map.134), channel_id=1, source_target_pairs={{0,1},{1,2},{2,3},{3,4},{4,5},{5,6},{6,7},{7,8},{8,9},{9,10},{10,1... | collective-permute-start | bytes 1376264 | tf_op jit(solution)/shard_map/ppermute | solution.py:249
  194.9 19.9 %collective-permute-start.50 = (bf16[64,3584]{1,0:T(8,128)(2,1)S(1)}, bf16[64,3584]{1,0:T(8,128)(2,1)S(1)}, u32[]{:S(2)}, u32[]{:S(2)}) collective-permute-start(bf16[64,3584]{1,0:T(8,128)(2,1)S(1)} %shard_map.141), channel_id=1, source_target_pairs={{0,15},{1,0},{2,1},{3,2},{4,3},{5,4},{6,5},{7,6},{8,7},{9,8},{10,9... | collective-permute-start | bytes 1376264 | tf_op jit(solution)/shard_map/ppermute | solution.py:243
  231.7 19.4 %collective-permute-start.45 = (bf16[64,3584]{1,0:T(8,128)(2,1)S(1)}, bf16[64,3584]{1,0:T(8,128)(2,1)S(1)}, u32[]{:S(2)}, u32[]{:S(2)}) collective-permute-start(bf16[64,3584]{1,0:T(8,128)(2,1)S(1)} %shard_map.136), channel_id=1, source_target_pairs={{0,1},{1,2},{2,3},{3,4},{4,5},{5,6},{6,7},{7,8},{8,9},{9,10},{10,1... | collective-permute-start | bytes 1376264 | tf_op jit(solution)/shard_map/ppermute | solution.py:249
  242.3 19.4 %collective-permute-start.38 = (bf16[64,3584]{1,0:T(8,128)(2,1)S(1)}, bf16[64,3584]{1,0:T(8,128)(2,1)S(1)}, u32[]{:S(2)}, u32[]{:S(2)}) collective-permute-start(bf16[64,3584]{1,0:T(8,128)(2,1)S(1)} %shard_map.129), channel_id=1, source_target_pairs={{0,15},{1,0},{2,1},{3,2},{4,3},{5,4},{6,5},{7,6},{8,7},{9,8},{10,9... | collective-permute-start | bytes 1376264 | tf_op jit(solution)/shard_map/ppermute | solution.py:243
  251.3 19.4 %collective-permute-start.46 = (bf16[64,3584]{1,0:T(8,128)(2,1)S(1)}, bf16[64,3584]{1,0:T(8,128)(2,1)S(1)}, u32[]{:S(2)}, u32[]{:S(2)}) collective-permute-start(bf16[64,3584]{1,0:T(8,128)(2,1)S(1)} %shard_map.137), channel_id=1, source_target_pairs={{0,1},{1,2},{2,3},{3,4},{4,5},{5,6},{6,7},{7,8},{8,9},{9,10},{10,1... | collective-permute-start | bytes 1376264 | tf_op jit(solution)/shard_map/ppermute | solution.py:249
  261.9 19.4 %collective-permute-start.39 = (bf16[64,3584]{1,0:T(8,128)(2,1)S(1)}, bf16[64,3584]{1,0:T(8,128)(2,1)S(1)}, u32[]{:S(2)}, u32[]{:S(2)}) collective-permute-start(bf16[64,3584]{1,0:T(8,128)(2,1)S(1)} %shard_map.130), channel_id=1, source_target_pairs={{0,15},{1,0},{2,1},{3,2},{4,3},{5,4},{6,5},{7,6},{8,7},{9,8},{10,9... | collective-permute-start | bytes 1376264 | tf_op jit(solution)/shard_map/ppermute | solution.py:243
  271.0 19.4 %collective-permute-start.47 = (bf16[64,3584]{1,0:T(8,128)(2,1)S(1)}, bf16[64,3584]{1,0:T(8,128)(2,1)S(1)}, u32[]{:S(2)}, u32[]{:S(2)}) collective-permute-start(bf16[64,3584]{1,0:T(8,128)(2,1)S(1)} %shard_map.138), channel_id=1, source_target_pairs={{0,1},{1,2},{2,3},{3,4},{4,5},{5,6},{6,7},{7,8},{8,9},{9,10},{10,1... | collective-permute-start | bytes 1376264 | tf_op jit(solution)/shard_map/ppermute | solution.py:249
  273.2 27.0 %collective-permute-start.54 = (bf16[64,3584]{1,0:T(8,128)(2,1)S(1)}, bf16[64,3584]{1,0:T(8,128)(2,1)S(1)}, u32[]{:S(2)}, u32[]{:S(2)}) collective-permute-start(bf16[64,3584]{1,0:T(8,128)(2,1)S(1)} %shard_map.145), channel_id=1, source_target_pairs={{0,15},{1,0},{2,1},{3,2},{4,3},{5,4},{6,5},{7,6},{8,7},{9,8},{10,9... | collective-permute-start | bytes 1376264 | tf_op jit(solution)/shard_map/ppermute | solution.py:243
  281.6 20.8 %collective-permute-start.40 = (bf16[64,3584]{1,0:T(8,128)(2,1)S(1)}, bf16[64,3584]{1,0:T(8,128)(2,1)S(1)}, u32[]{:S(2)}, u32[]{:S(2)}) collective-permute-start(bf16[64,3584]{1,0:T(8,128)(2,1)S(1)} %shard_map.131), channel_id=1, source_target_pairs={{0,15},{1,0},{2,1},{3,2},{4,3},{5,4},{6,5},{7,6},{8,7},{9,8},{10,9... | collective-permute-start | bytes 1376264 | tf_op jit(solution)/shard_map/ppermute | solution.py:243
  287.2 23.5 %collective-permute-start.62 = (bf16[64,3584]{1,0:T(8,128)(2,1)S(1)}, bf16[64,3584]{1,0:T(8,128)(2,1)S(1)}, u32[]{:S(2)}, u32[]{:S(2)}) collective-permute-start(bf16[64,3584]{1,0:T(8,128)(2,1)S(1)} %shard_map.153), channel_id=1, source_target_pairs={{0,1},{1,2},{2,3},{3,4},{4,5},{5,6},{6,7},{7,8},{8,9},{9,10},{10,1... | collective-permute-start | bytes 1376264 | tf_op jit(solution)/shard_map/ppermute | solution.py:249
  290.6 22.4 %collective-permute-start.48 = (bf16[64,3584]{1,0:T(8,128)(2,1)S(1)}, bf16[64,3584]{1,0:T(8,128)(2,1)S(1)}, u32[]{:S(2)}, u32[]{:S(2)}) collective-permute-start(bf16[64,3584]{1,0:T(8,128)(2,1)S(1)} %shard_map.139), channel_id=1, source_target_pairs={{0,17},{1,18},{2,19},{3,20},{4,21},{5,22},{6,23},{7,24},{8,25},{9,... | collective-permute-start | bytes 1376264 | tf_op jit(solution)/shard_map/ppermute | solution.py:235
  302.7 20.1 %collective-permute-start.41 = (bf16[64,3584]{1,0:T(8,128)(2,1)S(1)}, bf16[64,3584]{1,0:T(8,128)(2,1)S(1)}, u32[]{:S(2)}, u32[]{:S(2)}) collective-permute-start(bf16[64,3584]{1,0:T(8,128)(2,1)S(1)} %shard_map.132), channel_id=1, source_target_pairs={{0,31},{1,16},{2,17},{3,18},{4,19},{5,20},{6,21},{7,22},{8,23},{9,... | collective-permute-start | bytes 1376264 | tf_op jit(solution)/shard_map/ppermute | solution.py:235
  (47 other events, 748.0 us)
